TPU v7x, 256 devices: a whole 4x4x8 slice. The times are simulated.
256 devices in a mesh: row: 16 (over x_lo, z), col: 16 (over x_hi, y, core).
Axes of the slice: x: 4 (x_hi: 2, x_lo: 2; x = x_hi * 2 + x_lo), y: 4, z: 8, core: 2. Of those that a mesh axis runs over, the one named last changes fastest.
Arguments:
- points: bfloat16 [96, 1024, 1024], P('row', 'col')
- targets: bfloat16 [96, 1024, 1000], P('row', 'col'), may hold values from -6 to 6
- coeffs: float32 [96, 1024, 1000], P('row', 'col'), may hold values from -0.25 to 0.25
- block_inverse: float32 [96, 1024, 1024], P('row', 'col')
- block_order: int32 [96], replicated, may hold values from 0 to 95, each once
Outputs:
- coeffs_out: float32 [96, 1024, 1000], P('row', 'col')
All inputs are finite; a program needn't handle non-finite values.
Results may differ from a plain program's by a relative error of at most 0.0003.
Values may be sent and summed in bfloat16 or wider, within the bound.
A program may use at most 64 MiB of HBM per device.

v0:
```python
import jax
import jax.numpy as jnp
from jax import lax
from jax.sharding import PartitionSpec as P

STEPS = 2


ridge_weight = 1.0


def broadcast(value, axis, source):
    kept = jnp.where(lax.axis_index(axis) == source, value, 0).astype(value.dtype)
    return lax.psum(kept, axis)


def on_device(points, targets, coeffs, block_inverse, block_order):
    blocks_here, per_col, features = points.shape
    classes = targets.shape[2]
    my_row = lax.axis_index("row")
    my_col = lax.axis_index("col")
    flat_points = points.reshape(blocks_here * per_col, features)
    flat_wide = flat_points.astype(jnp.float32)
    point_squares = jnp.sum(flat_wide * flat_wide, axis=1)
    current = coeffs
    for sweep_step in range(STEPS):
        block_id = block_order[sweep_step]
        local_index = block_id % blocks_here
        owner_row = block_id // blocks_here
        own_slice = lax.dynamic_index_in_dim(points, local_index, 0, keepdims=False)
        full_block = lax.all_gather(own_slice, "col", axis=0, tiled=True)
        active = broadcast(full_block, "row", owner_row)
        active_wide = active.astype(jnp.float32)
        active_squares = jnp.sum(active_wide * active_wide, axis=1)
        inner = lax.dot_general(
            active, flat_points, (((1,), (1,)), ((), ())), preferred_element_type=jnp.float32
        )
        distance = active_squares[:, None] + point_squares[None, :] - 2.0 * inner
        tile_wide = jnp.exp(-distance * (0.5 / features))
        flat_current = current.reshape(blocks_here * per_col, classes)
        products = jnp.dot(
            tile_wide,
            flat_current,
            precision=lax.Precision.HIGHEST,
            preferred_element_type=jnp.float32,
        )
        summed = lax.psum(products, ("row", "col"))
        own_sum = lax.dynamic_slice_in_dim(summed, my_col * per_col, per_col, 0)
        previous = lax.dynamic_index_in_dim(current, local_index, 0, keepdims=False)
        wanted = lax.dynamic_index_in_dim(targets, local_index, 0, keepdims=False).astype(
            jnp.float32
        )
        residual = wanted - own_sum - ridge_weight * previous
        full_residual = lax.all_gather(residual, "col", axis=0, tiled=True)
        inverse_rows = lax.dynamic_index_in_dim(block_inverse, local_index, 0, keepdims=False)
        increment = jnp.dot(
            inverse_rows,
            full_residual,
            precision=lax.Precision.HIGHEST,
            preferred_element_type=jnp.float32,
        )
        updated = jnp.where(my_row == owner_row, previous + increment, previous)
        current = lax.dynamic_update_index_in_dim(current, updated, local_index, 0)
    return current


def solution(mesh):
    placed = (
        P("row", "col", None),
        P("row", "col", None),
        P("row", "col", None),
        P("row", "col", None),
        P(),
    )
    return jax.shard_map(
        on_device, mesh=mesh, in_specs=placed, out_specs=P("row", "col", None), check_vma=False
    )
```

profile of v0, /device:TPU:1, one launch (start us, length us, event | category | flops | bytes accessed | tf_op | source)
XLA Modules:
  0.0 974.0 jit_solution(10416053570746938592)
XLA Ops:
  6.5 1.5 copy.13
  8.1 0.6 fusion.40
  9.8 1.7 constant_dynamic-slice_fusion.2
  11.6 0.7 all-gather.11.cloned.1.call-update
  14.6 53.9 %all-gather.13.cloned.1.call-done = bf16[1,1024,1024]{2,1,0:T(8,128)(2,1)} async-done(((bf16[1,64,1024]{2,1,0:T(8,128)(2,1)}), bf16[1,1024,1024]{2,1,0:T(8,128)(2,1)}) %all-gather.13.cloned.1.call-update) | async-done | bytes 2097168 | tf_op jit(solution)/shard_map/all_gather | solution.py:31
  68.5 1.5 select_bitcast_fusion
  69.9 52.7 %all-gather.11.cloned.1.call-done = bf16[1,1024,1024]{2,1,0:T(8,128)(2,1)} async-done(((bf16[1,64,1024]{2,1,0:T(8,128)(2,1)}), bf16[1,1024,1024]{2,1,0:T(8,128)(2,1)}) %all-gather.11.cloned.1.call-update) | async-done | bytes 2097168 | tf_op jit(solution)/shard_map/all_gather | solution.py:31
  122.7 1.4 select_bitcast_fusion.1
  124.2 1.4 multiply_reduce_fusion.2
  125.7 143.2 %all-reduce.9.cloned.1.call-done = (bf16[1024,1024]{1,0:T(8,128)(2,1)}, bf16[1024,1024]{1,0:T(8,128)(2,1)}) async-done(((bf16[1024,1024]{1,0:T(8,128)(2,1)}, bf16[1024,1024]{1,0:T(8,128)(2,1)}), (bf16[1024,1024]{1,0:T(8,128)(2,1)}, bf16[1024,1024]{1,0:T(8,128)(2,1)})) %all-reduce.9.cloned.1.call-update) | async-done | bytes 4194320 | tf_op jit(solution)/shard_map/psum | solution.py:14
  268.9 2.2 multiply_reduce_fusion.1
  271.1 2.4 fusion.41
  273.5 8.6 fusion.7
  282.2 273.5 %all-reduce.5.cloned.1.call-done = f32[1024,1000]{1,0:T(8,128)} async-done(((f32[1024,1000]{1,0:T(8,128)}), f32[1024,1000]{1,0:T(8,128)}) %all-reduce.5.cloned.1.call-update) | async-done | bytes 4096016 | tf_op jit(solution)/shard_map/psum | solution.py:47
  555.7 1.7 fusion.29
  557.7 2.2 multiply_reduce_fusion
  560.0 3.6 fusion.42
  563.5 56.2 %all-gather.7.cloned.1.call-done = f32[1024,1000]{1,0:T(8,128)} async-done(((f32[64,1000]{1,0:T(8,128)}), f32[1024,1000]{1,0:T(8,128)}) %all-gather.7.cloned.1.call-update) | async-done | bytes 4096016 | tf_op jit(solution)/shard_map/all_gather | solution.py:54
  619.8 4.9 fusion.19
  624.7 8.6 fusion
  633.4 264.4 %all-reduce.7.cloned.1.call-done = f32[1024,1000]{1,0:T(8,128)} async-done(((f32[1024,1000]{1,0:T(8,128)}), f32[1024,1000]{1,0:T(8,128)}) %all-reduce.7.cloned.1.call-update) | async-done | bytes 4096016 | tf_op jit(solution)/shard_map/psum | solution.py:47
  897.8 1.7 fusion.28
  899.6 62.0 %all-gather.9.cloned.1.call-done = f32[1024,1000]{1,0:T(8,128)} async-done(((f32[64,1000]{1,0:T(8,128)}), f32[1024,1000]{1,0:T(8,128)}) %all-gather.9.cloned.1.call-update) | async-done | bytes 4096016 | tf_op jit(solution)/shard_map/all_gather | solution.py:54
  961.7 5.5 fusion.16
  (28 shorter events, 0.7 us)
Async XLA Ops:
  6.5 613.2 %copy-start = (f32[6,64,1024]{2,1,0:T(8,128)S(1)}, f32[6,64,1024]{2,1,0:T(8,128)}, u32[]{:S(2)}) copy-start(f32[6,64,1024]{2,1,0:T(8,128)} %param.8) | copy-start | bytes 4718596
  6.5 1.5 copy-start.5
  6.5 61.9 %all-gather.13.cloned.1.call-start = ((), (), s32[]{:S(2)}) async-start(), calls=%async_computation.5 | async-start | bytes 2228224 | tf_op jit(solution)/shard_map/all_gather | solution.py:31
  11.5 111.2 %all-gather.11.cloned.1.call-start = ((), (), s32[]{:S(2)}) async-start(), calls=%async_computation.4 | async-start | bytes 2228224 | tf_op jit(solution)/shard_map/all_gather | solution.py:31
  12.3 256.6 %all-reduce.9.cloned.1.call-start = ((), (), s32[]{:S(2)}) async-start(), calls=%async_computation.6 | async-start | bytes 8388608 | tf_op jit(solution)/shard_map/psum | solution.py:14
  124.2 431.6 %all-reduce.5.cloned.1.call-start = ((), (), s32[]{:S(2)}) async-start(), calls=%async_computation | async-start | bytes 8388608 | tf_op jit(solution)/shard_map/psum | solution.py:47
  268.9 2.2 copy-start.3
  282.1 337.6 %all-gather.7.cloned.1.call-start = ((), (), s32[]{:S(2)}) async-start(), calls=%async_computation.1 | async-start | bytes 4456448 | tf_op jit(solution)/shard_map/all_gather | solution.py:54
  557.5 340.4 %all-reduce.7.cloned.1.call-start = ((), (), s32[]{:S(2)}) async-start(), calls=%async_computation.2 | async-start | bytes 8388608 | tf_op jit(solution)/shard_map/psum | solution.py:47
  557.7 2.3 copy-start.2
  619.8 5.0 copy-start.4
  624.7 274.9 %copy-start.1 = (f32[6,64,1000]{2,1,0:T(8,128)}, f32[6,64,1000]{2,1,0:T(8,128)S(1)}, u32[]{:S(2)}) copy-start(f32[6,64,1000]{2,1,0:T(8,128)S(1)} %fusion.19) | copy-start | bytes 4608004
  633.4 328.3 %all-gather.9.cloned.1.call-start = ((), (), s32[]{:S(2)}) async-start(), calls=%async_computation.3 | async-start | bytes 4456448 | tf_op jit(solution)/shard_map/all_gather | solution.py:54
Sparse Core Ops, SparseCore 0:
  11.6 56.7 all-gather.12
  71.2 51.4 all-gather.10
  125.4 143.4 all-reduce.8
  282.3 273.4 all-reduce.4
  558.7 61.0 all-gather.6
  633.5 264.3 all-reduce.6
  900.6 61.0 all-gather.8
where the time goes:
time: 974 us
  waiting for transfers between devices  907 us (93%)
  matrix products  33.7 us (3%)
  between operations  17 us (2%)
  other arithmetic  12.2 us (1%)
    psum x2, waiting for transfers between devices, on_device(): summed = lax.psum(products, ('row', 'col'))  538 us
    psum x1, waiting for transfers between devices, broadcast(): return lax.psum(kept, axis)  143 us
    all_gather x2, waiting for transfers between devices, on_device(): full_residual = lax.all_gather(residual, 'col', axis=0, tiled=True)  118 us
    all_gather x2, waiting for transfers between devices, on_device(): full_block = lax.all_gather(own_slice, 'col', axis=0, tiled=True)  107 us
  transfers between devices with their start and end apart: 7, of which 7 were waited for; matrix products, arithmetic and copies ran while one was open for 1% of the time, Pallas kernels for 0%

commit v1 on v0

v1 whole, which is shorter than its diff:
```python
import functools

import jax
import jax.numpy as jnp
from jax import lax
from jax.experimental import pallas as pl
from jax.experimental.pallas import tpu as pltpu
from jax.sharding import PartitionSpec as P

MESH = pl.DeviceIdType.MESH
ANY = pl.BlockSpec(memory_space=pl.ANY)
VMEM = pl.BlockSpec(memory_space=pltpu.VMEM)
DMA = pltpu.SemaphoreType.DMA

ridge_weight = 1.0


def place():
    row, col = lax.axis_index("row"), lax.axis_index("col")
    return col // 8, row // 8, (col // 2) % 4, row % 8, col % 2


def device(x, y, z, core):
    return (x % 2) * 8 + z, (x // 2) * 8 + y * 2 + core


class Group:
    def __init__(self, kind):
        x_hi, x_lo, y, z, core = place()
        row, col = lax.axis_index("row"), lax.axis_index("col")
        x = x_hi * 2 + x_lo
        self.size, self.me, self.at = {
            "row": (16, row, lambda i: (i, col)),
            "col": (16, col, lambda i: (row, i)),
            "x": (4, x, lambda i: device(i, y, z, core)),
            "y": (4, y, lambda i: device(x, i, z, core)),
            "z": (8, z, lambda i: device(x, y, i, core)),
            "core": (2, core, lambda i: device(x, y, z, i)),
        }[kind]

    def after(self, step):
        return lax.rem(self.me + step, self.size)

    def before(self, step):
        return lax.rem(self.me + self.size - step, self.size)


def greet(groups):
    barrier = pltpu.get_barrier_semaphore()
    for group in groups:
        for step in range(1, group.size):
            pl.semaphore_signal(barrier, inc=1, device_id=group.at(group.after(step)), device_id_type=MESH)
    pl.semaphore_wait(barrier, sum(group.size - 1 for group in groups))


def send_all(group, source, target, send_sem, recv_sem):
    copies = []
    for step in range(1, group.size):
        to = group.after(step)
        out = pltpu.make_async_remote_copy(
            src_ref=source(to), dst_ref=target(group.me, step), send_sem=send_sem(step), recv_sem=recv_sem(step),
            device_id=group.at(to), device_id_type=MESH)
        out.start()
        back = pltpu.make_async_remote_copy(
            src_ref=source(to), dst_ref=target(group.before(step), step), send_sem=send_sem(step),
            recv_sem=recv_sem(step), device_id=group.at(to), device_id_type=MESH)
        copies.append((out, back))
    return copies


def arrived(copies):
    for _, back in copies:
        back.wait_recv()


def sent(copies):
    for out, _ in copies:
        out.wait_send()


def exchange_start(group, mode, source, target, send_sems, recv_sems, own_sem):
    pick = (lambda i: source.at[i]) if mode == "each" else (lambda i: source)
    own = pltpu.make_async_copy(pick(group.me), target.at[group.me], own_sem)
    own.start()
    copies = send_all(group, pick, lambda i, step: target.at[i], lambda s: send_sems.at[s - 1], lambda s: recv_sems.at[s - 1])
    return own, copies


def exchange_wait(handle):
    own, copies = handle
    own.wait()
    arrived(copies)
    sent(copies)


def exchange_kernel(plan, *refs):
    count = len(plan)
    sources, targets = refs[:count], refs[count:2 * count]
    send_sems, recv_sems, own_sems = refs[2 * count:]
    groups = {kind: Group(kind) for kind, _ in plan}
    greet(list(groups.values()))
    handles = [
        exchange_start(groups[kind], mode, sources[i], targets[i], send_sems.at[i], recv_sems.at[i], own_sems.at[i])
        for i, (kind, mode) in enumerate(plan)
    ]
    for handle in handles:
        exchange_wait(handle)


def exchange(arrays, plan, collective_id):
    shapes = [a.shape if mode == "each" else (16, *a.shape) for a, (_, mode) in zip(arrays, plan)]
    return pl.pallas_call(
        functools.partial(exchange_kernel, tuple(plan)),
        out_shape=[jax.ShapeDtypeStruct(s, a.dtype) for s, a in zip(shapes, arrays)],
        in_specs=[ANY] * len(arrays),
        out_specs=[ANY] * len(arrays),
        scratch_shapes=[DMA((len(arrays), 15)), DMA((len(arrays), 15)), DMA((len(arrays),))],
        compiler_params=pltpu.CompilerParams(collective_id=collective_id, has_side_effects=True),
    )(*arrays)


def gather_kernel(chunk, full, send_sems, recv_sems, own_sem):
    x_hi, x_lo, y, z, core = place()
    gx, gy, gz, gc = Group("x"), Group("y"), Group("z"), Group("core")
    greet([gx, gy, gz, gc])

    def piece(i):
        quarter, lanes = i // 2, i % 2
        return full.at[core, x_hi, y, x_lo, quarter // 2, pl.ds(pl.multiple_of((quarter % 2) * 16, 16), 16),
                       pl.ds(pl.multiple_of(lanes * 512, 512), 512)]

    def sems(base):
        return (lambda s: send_sems.at[base + s - 1]), (lambda s: recv_sems.at[base + s - 1])

    own = pltpu.make_async_copy(chunk, piece(z), own_sem)
    own.start()
    along_z = send_all(gz, lambda i: chunk, lambda i, s: piece(i), *sems(0))
    own.wait()
    arrived(along_z)
    x_first = send_all(gx, lambda i: full.at[core, x_hi, y, x_lo, 0], lambda i, s: full.at[core, i // 2, y, i % 2, 0], *sems(7))
    y_first = send_all(gy, lambda i: full.at[core, x_hi, y, x_lo, 1], lambda i, s: full.at[core, x_hi, i, x_lo, 1], *sems(10))
    arrived(x_first)
    y_last = send_all(gy, lambda i: full.at[core, :, y, :, 0], lambda i, s: full.at[core, :, i, :, 0], *sems(13))
    arrived(y_first)
    x_last = send_all(gx, lambda i: full.at[core, x_hi, :, x_lo, 1], lambda i, s: full.at[core, i // 2, :, i % 2, 1], *sems(16))
    arrived(y_last)
    across_0 = send_all(gc, lambda i: full.at[core, :, :, :, 0], lambda i, s: full.at[i, :, :, :, 0], *sems(19))
    arrived(x_last)
    across_1 = send_all(gc, lambda i: full.at[core, :, :, :, 1], lambda i, s: full.at[i, :, :, :, 1], *sems(20))
    arrived(across_0)
    arrived(across_1)
    for copies in (along_z, x_first, y_first, y_last, x_last, across_0, across_1):
        sent(copies)


def gather_points(chunk, collective_id):
    return pl.pallas_call(
        gather_kernel,
        out_shape=jax.ShapeDtypeStruct((2, 2, 4, 2, 2, 32, 1024), chunk.dtype),
        in_specs=[ANY],
        out_specs=ANY,
        scratch_shapes=[DMA((21,)), DMA((21,)), DMA],
        compiler_params=pltpu.CompilerParams(collective_id=collective_id, has_side_effects=True),
    )(chunk)


def reduce_kernel(parts, inverse, wanted, total, inverse_out, wanted_out, held, core_in, x_in, y_in, x_sum, y_sum, y_in_2,
                  x_in_2, z_sum, z_in, send_sems, recv_sems, own_sem, more_send, more_recv, more_own):
    x_hi, x_lo, y, z, core = place()
    gx, gy, gz, gc, gr = Group("x"), Group("y"), Group("z"), Group("core"), Group("row")
    greet([gx, gy, gz, gc, gr])

    def sems(base):
        return (lambda s: send_sems.at[base + s - 1]), (lambda s: recv_sems.at[base + s - 1])

    across = send_all(gc, lambda i: parts.at[i], lambda i, s: core_in, *sems(0))
    own = pltpu.make_async_copy(parts.at[core], held, own_sem)
    own.start()
    more = [
        exchange_start(gr, "each", inverse, inverse_out, more_send.at[0], more_recv.at[0], more_own.at[0]),
        exchange_start(gr, "each", wanted, wanted_out, more_send.at[1], more_recv.at[1], more_own.at[1]),
    ]
    own.wait()
    arrived(across)

    def add(i, carry):
        held[i // 4, i % 4] += core_in[i // 4, i % 4]
        return carry

    lax.fori_loop(0, 8, add, 0)
    x_first = send_all(gx, lambda i: held.at[i // 2, :, i % 2, 0], lambda i, s: x_in.at[s - 1], *sems(1))
    y_first = send_all(gy, lambda i: held.at[:, i, :, 1], lambda i, s: y_in.at[s - 1], *sems(4))
    arrived(x_first)
    x_sum[...] = held[x_hi, :, x_lo, 0] + x_in[0] + x_in[1] + x_in[2]
    y_last = send_all(gy, lambda i: x_sum.at[i], lambda i, s: y_in_2.at[s - 1], *sems(7))
    arrived(y_first)
    y_sum[...] = held[:, y, :, 1] + y_in[0] + y_in[1] + y_in[2]
    x_last = send_all(gx, lambda i: y_sum.at[i // 2, i % 2], lambda i, s: x_in_2.at[s - 1], *sems(10))
    arrived(y_last)
    z_sum[0] = x_sum[y] + y_in_2[0] + y_in_2[1] + y_in_2[2]
    arrived(x_last)
    z_sum[1] = y_sum[x_hi, x_lo] + x_in_2[0] + x_in_2[1] + x_in_2[2]

    def slab(i):
        return z_sum.at[i // 4, pl.ds(pl.multiple_of((i % 4) * 64, 64), 64)]

    along_z = send_all(gz, slab, lambda i, s: z_in.at[s - 1], *sems(13))
    arrived(along_z)
    result = z_sum[z // 4, pl.ds(pl.multiple_of((z % 4) * 64, 64), 64)]
    for i in range(7):
        result += z_in[i]
    total[...] = result
    for copies in (across, x_first, y_first, y_last, x_last, along_z):
        sent(copies)
    for handle in more:
        exchange_wait(handle)


def reduce_parts(parts, inverse, wanted, collective_id):
    f32 = jnp.float32
    return pl.pallas_call(
        reduce_kernel,
        out_shape=[jax.ShapeDtypeStruct((64, 128), f32), jax.ShapeDtypeStruct(inverse.shape, f32),
                   jax.ShapeDtypeStruct(wanted.shape, f32)],
        in_specs=[ANY, ANY, ANY],
        out_specs=[VMEM, ANY, ANY],
        scratch_shapes=[
            pltpu.VMEM((2, 4, 2, 2, 256, 128), f32),
            pltpu.VMEM((2, 4, 2, 2, 256, 128), f32),
            pltpu.VMEM((3, 4, 256, 128), f32),
            pltpu.VMEM((3, 2, 2, 256, 128), f32),
            pltpu.VMEM((4, 256, 128), f32),
            pltpu.VMEM((2, 2, 256, 128), f32),
            pltpu.VMEM((3, 256, 128), f32),
            pltpu.VMEM((3, 256, 128), f32),
            pltpu.VMEM((2, 256, 128), f32),
            pltpu.VMEM((7, 64, 128), f32),
            DMA((20,)), DMA((20,)), DMA, DMA((2, 15)), DMA((2, 15)), DMA((2,)),
        ],
        compiler_params=pltpu.CompilerParams(collective_id=collective_id, has_side_effects=True, vmem_limit_bytes=40 * 2**20),
    )(parts, inverse, wanted)


def squares(points):
    wide = points.astype(jnp.float32)
    return jnp.sum(wide * wide, axis=-1)


def kern(left, right):
    inner = lax.dot_general(left, right, (((1,), (1,)), ((), ())), preferred_element_type=jnp.float32)
    distance = squares(left)[:, None] + squares(right)[None, :] - 2.0 * inner
    return jnp.exp(-distance * (0.5 / left.shape[1]))


def product(left, right, contract):
    return lax.dot_general(left, right, (contract, ((), ())), precision=lax.Precision.HIGH,
                           preferred_element_type=jnp.float32)


def on_device(points, targets, coeffs, block_inverse, block_order):
    blocks_here, per_col, features = points.shape
    classes = targets.shape[2]
    f32 = jnp.float32
    my_row = lax.axis_index("row")
    x_lo = my_row // 8
    ids = [block_order[0], block_order[1]]
    local = [b % blocks_here for b in ids]
    owner = [b // blocks_here for b in ids]

    def pick(array, step):
        return lax.dynamic_index_in_dim(array, local[step], 0, keepdims=False)

    def both(array):
        return jnp.stack([pick(array, 0), pick(array, 1)])

    own_points = both(points).reshape(2, 4, 16, 2, 512).transpose(0, 1, 3, 2, 4).reshape(16, 16, 512)
    (offers,) = exchange([own_points], [("row", "each")], 0)
    my_owner = jnp.where(x_lo == 0, owner[0], owner[1])
    chunk = lax.dynamic_index_in_dim(offers, my_owner, 0, keepdims=False)
    active = gather_points(chunk, 1)

    inverse_offer = both(block_inverse).reshape(16, 8, 1024)
    previous = both(coeffs)
    need = both(targets).astype(f32) - ridge_weight * previous
    need = jnp.pad(need, ((0, 0), (0, 0), (0, 1024 - classes)))
    wanted_offer = need.transpose(2, 0, 1).reshape(16, 64, 128)

    flat_points = points.reshape(blocks_here * per_col, features)
    flat_coeffs = jnp.pad(coeffs.reshape(blocks_here * per_col, classes), ((0, 0), (0, 1024 - classes)))
    tile = kern(active.reshape(2048, features), flat_points)
    parts = product(flat_coeffs, tile, ((0,), (1,)))
    parts = parts.reshape(1024, 16, 128).transpose(1, 0, 2).reshape(2, 2, 4, 2, 2, 256, 128)
    total, inverse_got, wanted_got = reduce_parts(parts, inverse_offer, wanted_offer, 2)

    inverse_chunk = lax.dynamic_index_in_dim(inverse_got, my_owner, 0, keepdims=False)
    wanted = jnp.concatenate([
        lax.dynamic_index_in_dim(wanted_got, owner[0], 0, keepdims=False)[:, :64],
        lax.dynamic_index_in_dim(wanted_got, owner[1], 0, keepdims=False)[:, 64:],
    ], axis=1)
    residual = wanted - total
    residual_all, inverse_all = exchange([residual, inverse_chunk], [("col", "all"), ("row", "all")], 3)
    inverse = inverse_all.reshape(2, 64, 1024)
    residual_all = residual_all.reshape(16, 64, 2, 64).transpose(2, 1, 0, 3).reshape(2, 64, 1024)

    delta_1 = product(residual_all[0], inverse[0], ((1,), (1,)))
    (delta_all,) = exchange([jnp.pad(delta_1, ((0, 0), (0, 64)))], [("col", "all")], 4)
    delta_all = delta_all[:, :, :64].transpose(1, 0, 2).reshape(64, 1024)
    ordered = active.transpose(3, 1, 2, 0, 4, 5, 6).reshape(2, 1024, features)
    between = kern(ordered[1], ordered[0])
    residual_2 = residual_all[1] - product(delta_all, between, ((1,), (1,)))
    delta_2 = product(residual_2, inverse[1], ((1,), (1,)))
    (deltas,) = exchange([jnp.concatenate([delta_1, delta_2], axis=1)], [("row", "all")], 5)
    deltas = deltas.reshape(1024, 2, 64).transpose(1, 2, 0)[:, :, :classes]

    current = coeffs
    for step in range(2):
        before = lax.dynamic_index_in_dim(current, local[step], 0, keepdims=False)
        updated = jnp.where(my_row == owner[step], before + deltas[step], before)
        current = lax.dynamic_update_index_in_dim(current, updated, local[step], 0)
    return current


def solution(mesh):
    placed = (
        P("row", "col", None),
        P("row", "col", None),
        P("row", "col", None),
        P("row", "col", None),
        P(),
    )
    return jax.shard_map(
        on_device, mesh=mesh, in_specs=placed, out_specs=P("row", "col", None), check_vma=False
    )
```

time: 974 us -> 229 us (0.24)
  waiting for transfers between devices: 907 us -> 0 us
  Pallas kernels: 0 us -> 161 us
  local copies, waits for them, and re-layouts: 3.94 us -> 29.2 us
  between operations: 17 us -> 4.13 us
    psum x3 -> x0, waiting for transfers between devices: 681 us -> none  [the longest x2 538 us: on_device(): summed = lax.psum(products, ('row', 'col'))]
    all_gather x4 -> x0, waiting for transfers between devices: 225 us -> none  [the longest x2 118 us: on_device(): full_residual = lax.all_gather(residual, 'col', axis=0, tiled=True)]
    pallas_call x0 -> x6, Pallas kernels: none -> 161 us  [the longest x4 66.5 us: exchange(): pl.pallas_call(functools.partial(exchange_kernel, tuple(plan)), out_shape...]
    reshape x0 -> x10, local copies, waits for them, and re-layouts: none -> 12.5 us  [the longest x1 4.07 us: on_device(): parts.reshape(1024, 16, 128).transpose(1, 0, 2)]
  transfers between devices with their start and end apart: 7 -> 0, of which waited for: 7 -> 0; matrix products, arithmetic and copies ran while one was open for 1% -> 0% of each run, Pallas kernels for 0% -> 0%
where the time goes in v1:
time: 229 us; the launch traced here: 228 us
  Pallas kernels  161 us (70%)
  local copies, waits for them, and re-layouts  29.2 us (13%)
  matrix products  28.7 us (13%)
  other arithmetic  5.25 us (2%)
  between operations  4.13 us (2%)
    pallas_call x4, Pallas kernels, exchange(): pl.pallas_call(functools.partial(exchange_kernel, tuple(plan)), out_shape...  66.5 us
    pallas_call x1, Pallas kernels, reduce_parts(): pl.pallas_call(reduce_kernel, out_shape=[jax.ShapeDtypeStruct((64, 128),...  60.4 us
    pallas_call x1, Pallas kernels, gather_points(): pl.pallas_call(gather_kernel, out_shape=jax.ShapeDtypeStruct((2, 2, 4, 2,...  33.9 us
    dot_general x4, matrix products, product(): lax.dot_general(left, right, (contract, ((), ())), precision=lax.Precisio...  18 us
    dot_general x2, matrix products, kern(): lax.dot_general(left, right, (((1,), (1,)), ((), ())), preferred_element_...  10.7 us
    unnamed x15, local copies, waits for them, and re-layouts  6.02 us

profile of v1, /device:TPU:1, one launch (start us, length us, event | category | flops | bytes accessed | tf_op | source)
XLA Modules:
  0.0 228.1 jit_solution(13779766055492386868)
XLA Ops:
  0.0 1.5 copy.45
  4.4 15.7 %shard_map.55 = bf16[16,16,512]{2,1,0:T(8,128)(2,1)} custom-call(bf16[16,16,512]{2,1,0:T(8,128)(2,1)} %bitcast.72), custom_call_target="tpu_custom_call" | custom-call | tf_op jit(solution)/shard_map/pallas_call | solution.py:112
  22.6 1.3 dynamic-slice_bitcast_fusion.3.chunk
  24.0 33.9 %shard_map.56 = bf16[2,2,4,2,2,32,1024]{6,5,4,3,2,1,0:T(8,128)(2,1)} custom-call(bf16[16,512]{1,0:T(8,128)(2,1)} %dynamic-slice_bitcast_fusion.3.chunk), custom_call_target="tpu_custom_call" | custom-call | tf_op jit(solution)/shard_map/pallas_call | solution.py:157
  57.9 6.4 %fusion.41 = f32[2048,384]{1,0:T(8,128)} fusion(bf16[2048,1024]{1,0:T(8,128)(2,1)} %bitcast.62, bf16[384,1024]{1,0:T(8,128)(2,1)S(1)} %bitcast.71), kind=kOutput, calls=%fused_computation.67 | convolution fusion | flops 1610612736 | bytes 8126464 | tf_op jit(solution)/shard_map/dot_general | solution.py:250
  65.5 12.7 %convolution_bitcast_fusion = f32[128,16,8,128]{3,2,1,0:T(8,128)S(1)} fusion(f32[2048,384]{1,0:T(8,128)} %fusion.41, f32[384]{0:T(512)S(1)} %add.99, f32[2048]{0:T(1024)S(1)} %add.97, f32[384,1000]{1,0:T(8,128)S(1)} %bitcast.65), kind=kOutput, calls=%fused_computation.11 | convolution fusion | flops 4835770368 | bytes 13080064 | tf_op jit(solution)/shard_map/dot_general | solution.py:256
  78.3 4.1 %copy.40 = f32[128,16,8,128]{3,2,0,1:T(8,128)} copy(f32[128,16,8,128]{3,2,1,0:T(8,128)S(1)} %convolution_bitcast_fusion) | data formatting | bytes 16777216 | tf_op jit(solution)/shard_map/reshape | solution.py:292
  82.4 1.0 constant_dynamic-slice_fusion.2
  83.5 1.2 reshape.85
  84.7 1.6 copy.28.wanted
  86.3 1.1 constant_dynamic-slice_fusion.4
  87.5 3.4 %copy-done = f32[128,16,8,128]{3,2,0,1:T(8,128)S(1)} copy-done((f32[128,16,8,128]{3,2,0,1:T(8,128)S(1)}, f32[128,16,8,128]{3,2,0,1:T(8,128)}, u32[]{:S(2)}) %copy-start) | copy-done | bytes 8388632
  90.9 60.4 %shard_map.57 = (f32[64,128]{1,0:T(8,128)S(1)}, f32[16,8,1024]{2,1,0:T(8,128)S(1)}, f32[16,64,128]{2,1,0:T(8,128)S(1)}) custom-call(f32[2,2,4,2,2,256,128]{6,5,4,3,2,1,0:T(8,128)S(1)} %bitcast.60, f32[16,8,1024]{2,1,0:T(8,128)S(1)} %bitcast.61, f32[16,64,128]{2,1,0:T(8,128)S(1)} %copy.28.wanted), custom_call_target="tpu_custom_call" | custom-call | tf_op jit(solution)/shard_map/pallas_call | solution.py:221
  152.7 19.0 %shard_map.58 = (f32[16,64,128]{2,1,0:T(8,128)}, f32[16,8,1024]{2,1,0:T(8,128)}) custom-call(f32[64,128]{1,0:T(8,128)} %maximum_subtract_fusion.1.refs_0_, f32[8,1024]{1,0:T(8,128)} %dynamic-slice_bitcast_fusion.refs_1_), custom_call_target="tpu_custom_call" | custom-call | tf_op jit(solution)/shard_map/pallas_call | solution.py:112
  171.7 1.7 reshape.86
  175.2 13.3 %shard_map.59 = f32[16,64,128]{2,1,0:T(8,128)} custom-call(f32[64,128]{1,0:T(8,128)} %pad.14.refs_0_), custom_call_target="tpu_custom_call" | custom-call | tf_op jit(solution)/shard_map/pallas_call | solution.py:112
  188.4 1.1 slice_bitcast_fusion
  190.2 2.7 %fusion.38 = (bf16[1,2,4,2,2,32,1024]{6,5,4,0,2,1,3:T(8,128)(2,1)S(1)}, bf16[1,2,4,2,2,32,1024]{6,5,4,0,2,1,3:T(8,128)(2,1)S(1)}) fusion(bf16[2,2,4,2,2,32,1024]{6,5,4,0,2,1,3:T(8,128)(2,1)} %bitcast.63), kind=kLoop, calls=%fused_computation.64 | loop fusion | bytes 8388608 | tf_op jit(solution)/shard_map/slice | solution.py:309
  193.3 4.3 %fusion.42 = f32[1024,1024]{1,0:T(8,128)} fusion(bf16[1024,1024]{1,0:T(8,128)(2,1)S(1)} %bitcast.69, bf16[1024,1024]{1,0:T(8,128)(2,1)S(1)} %bitcast.70), kind=kOutput, calls=%fused_computation.68 | convolution fusion | flops 2147483648 | bytes 8388608 | tf_op jit(solution)/shard_map/dot_general | solution.py:250
  198.7 4.8 %fusion.22 = f32[64,1024]{1,0:T(8,128)S(1)} fusion(f32[64,1024]{1,0:T(8,128)S(1)} %squeeze.57, f32[64,1024]{1,0:T(8,128)S(1)} %reshape.87, f32[1024,1024]{1,0:T(8,128)} %fusion.42, f32[1024]{0:T(1024)S(1)} %add.106, f32[1024]{0:T(1024)S(1)} %add.104), kind=kOutput, calls=%fused_computation.28 | convolution fusion | flops 407961600 | bytes 4988928 | tf_op jit(solution)/shard_map/dot_general | solution.py:256
  204.5 18.6 %shard_map.60 = f32[16,64,128]{2,1,0:T(8,128)} custom-call(f32[64,128]{1,0:T(8,128)} %pad_maximum_fusion.2.refs_0_), custom_call_target="tpu_custom_call" | custom-call | tf_op jit(solution)/shard_map/pallas_call | solution.py:112
  223.1 1.7 reshape.89
  225.3 1.1 copy-done.3
  226.5 1.7 fusion.26
  (48 shorter events, 9.9 us)
Async XLA Ops:
  0.0 3.4 %copy-start.4 = (bf16[6,64,1024]{2,1,0:T(8,128)(2,1)S(1)}, bf16[6,64,1024]{2,1,0:T(8,128)(2,1)}, u32[]{:S(2)}) copy-start(bf16[6,64,1024]{2,1,0:T(8,128)(2,1)} %param.5) | copy-start | bytes 2359300
  0.0 1.5 copy-start.6
  57.9 6.4 %copy-start.1 = (bf16[2,2,4,2,2,32,1024]{6,5,4,3,2,1,0:T(8,128)(2,1)S(1)}, bf16[2,2,4,2,2,32,1024]{6,5,4,3,2,1,0:T(8,128)(2,1)}, u32[]{:S(2)}) copy-start(bf16[2,2,4,2,2,32,1024]{6,5,4,3,2,1,0:T(8,128)(2,1)} %shard_map.56) | copy-start | bytes 12582916
  87.5 3.4 %copy-start = (f32[128,16,8,128]{3,2,0,1:T(8,128)S(1)}, f32[128,16,8,128]{3,2,0,1:T(8,128)}, u32[]{:S(2)}) copy-start(f32[128,16,8,128]{3,2,0,1:T(8,128)} %copy.40) | copy-start | bytes 25165828
  171.7 2.6 %copy-start.5 = (f32[16,8,1024]{2,1,0:T(8,128)S(1)}, f32[16,8,1024]{2,1,0:T(8,128)}, u32[]{:S(2)}) copy-start(f32[16,8,1024]{2,1,0:T(8,128)} %get-tuple-element.14) | copy-start | bytes 1572868
  193.3 4.3 %copy-start.2 = (bf16[2,2,4,2,2,32,1024]{6,5,4,3,2,1,0:T(8,128)(2,1)S(1)}, bf16[2,2,4,2,2,32,1024]{6,5,4,3,2,1,0:T(8,128)(2,1)}, u32[]{:S(2)}) copy-start(bf16[2,2,4,2,2,32,1024]{6,5,4,3,2,1,0:T(8,128)(2,1)} %shard_map.56) | copy-start | bytes 12582916
  225.3 1.1 copy-start.3

commit v2 on v1

v2 whole, which is shorter than its diff:
```python
import functools

import jax
import jax.numpy as jnp
from jax import lax
from jax.experimental import pallas as pl
from jax.experimental.pallas import tpu as pltpu
from jax.sharding import PartitionSpec as P

MESH = pl.DeviceIdType.MESH
ANY = pl.BlockSpec(memory_space=pl.ANY)
VMEM = pl.BlockSpec(memory_space=pltpu.VMEM)
DMA = pltpu.SemaphoreType.DMA

ridge_weight = 1.0


def place():
    row, col = lax.axis_index("row"), lax.axis_index("col")
    return col // 8, row // 8, (col // 2) % 4, row % 8, col % 2


def device(x, y, z, core):
    return (x % 2) * 8 + z, (x // 2) * 8 + y * 2 + core


class Group:
    def __init__(self, kind):
        x_hi, x_lo, y, z, core = place()
        row, col = lax.axis_index("row"), lax.axis_index("col")
        x = x_hi * 2 + x_lo
        self.size, self.me, self.at = {
            "row": (16, row, lambda i: (i, col)),
            "col": (16, col, lambda i: (row, i)),
            "x": (4, x, lambda i: device(i, y, z, core)),
            "y": (4, y, lambda i: device(x, i, z, core)),
            "z": (8, z, lambda i: device(x, y, i, core)),
            "core": (2, core, lambda i: device(x, y, z, i)),
        }[kind]

    def after(self, step):
        return lax.rem(self.me + step, self.size)

    def before(self, step):
        return lax.rem(self.me + self.size - step, self.size)


def greet(groups):
    barrier = pltpu.get_barrier_semaphore()
    for group in groups:
        for step in range(1, group.size):
            pl.semaphore_signal(barrier, inc=1, device_id=group.at(group.after(step)), device_id_type=MESH)
    pl.semaphore_wait(barrier, sum(group.size - 1 for group in groups))


def send_all(group, source, target, send_sem, recv_sem):
    copies = []
    for step in range(1, group.size):
        to = group.after(step)
        out = pltpu.make_async_remote_copy(
            src_ref=source(to), dst_ref=target(group.me, step), send_sem=send_sem(step), recv_sem=recv_sem(step),
            device_id=group.at(to), device_id_type=MESH)
        out.start()
        back = pltpu.make_async_remote_copy(
            src_ref=source(to), dst_ref=target(group.before(step), step), send_sem=send_sem(step),
            recv_sem=recv_sem(step), device_id=group.at(to), device_id_type=MESH)
        copies.append((out, back))
    return copies


def arrived(copies):
    for _, back in copies:
        back.wait_recv()


def sent(copies):
    for out, _ in copies:
        out.wait_send()


def exchange_start(group, mode, source, target, send_sems, recv_sems, own_sem):
    pick = (lambda i: source.at[i]) if mode == "each" else (lambda i: source)
    own = pltpu.make_async_copy(pick(group.me), target.at[group.me], own_sem)
    own.start()
    copies = send_all(group, pick, lambda i, step: target.at[i], lambda s: send_sems.at[s - 1], lambda s: recv_sems.at[s - 1])
    return own, copies


def exchange_wait(handle):
    own, copies = handle
    own.wait()
    arrived(copies)
    sent(copies)


def exchange_kernel(plan, *refs):
    count = len(plan)
    sources, targets = refs[:count], refs[count:2 * count]
    send_sems, recv_sems, own_sems = refs[2 * count:]
    groups = {kind: Group(kind) for kind, _ in plan}
    greet(list(groups.values()))
    handles = [
        exchange_start(groups[kind], mode, sources[i], targets[i], send_sems.at[i], recv_sems.at[i], own_sems.at[i])
        for i, (kind, mode) in enumerate(plan)
    ]
    for handle in handles:
        exchange_wait(handle)


def exchange(arrays, plan, collective_id):
    shapes = [a.shape if mode == "each" else (16, *a.shape) for a, (_, mode) in zip(arrays, plan)]
    return pl.pallas_call(
        functools.partial(exchange_kernel, tuple(plan)),
        out_shape=[jax.ShapeDtypeStruct(s, a.dtype) for s, a in zip(shapes, arrays)],
        in_specs=[ANY] * len(arrays),
        out_specs=[ANY] * len(arrays),
        scratch_shapes=[DMA((len(arrays), 15)), DMA((len(arrays), 15)), DMA((len(arrays),))],
        compiler_params=pltpu.CompilerParams(collective_id=collective_id, has_side_effects=True),
    )(*arrays)


F32 = jnp.float32
NT = (((1,), (1,)), ((), ()))
LIMIT = 32000.0
DOTS = dict(preferred_element_type=jnp.float32)


def code(pieces, slot):
    top = None
    for piece in pieces:
        size = jnp.abs(piece())
        top = size if top is None else jnp.maximum(top, size)
    top = jnp.max(top, axis=0, keepdims=True)
    level = jnp.ceil(jnp.log2(jnp.maximum(top, 1e-30)) * 16.0)
    row = jnp.broadcast_to(level, (16, 128))
    factor = LIMIT * jnp.exp2(row[0:1] * (-1.0 / 16.0))
    at = 0
    for piece in pieces:
        value = jnp.round(piece() * factor)
        rows = value.shape[0]
        slot[at:at + rows, :] = value.astype(jnp.int32).astype(jnp.int16)
        at += rows
    slot[at:at + 16, :] = row.astype(jnp.int32).astype(jnp.int16)


def wide(value):
    return value.astype(jnp.int32).astype(jnp.float32)


def scale_of(slot, rows):
    return jnp.exp2(wide(slot[rows:rows + 16, :])[0:1] * (1.0 / 16.0)) * (1.0 / LIMIT)


def decode(slot, rows):
    return wide(slot[0:rows, :]) * scale_of(slot, rows)


def squares_of(rows):
    value = rows.astype(F32)
    return jnp.sum(value * value, axis=1, keepdims=True)


def halves(value):
    high = value.astype(jnp.bfloat16)
    return high, (value - high.astype(F32)).astype(jnp.bfloat16)


def main_kernel(owner, chunk, points, squares_row, weights, inverse, wanted, out,
                full, tile, mine, theirs, core_in, x_out, x_in, y_out, y_in, u, v, y_out_2, y_in_2, x_out_2, x_in_2, z_sum,
                z_out, z_in, inverse_in, inverse_all, wanted_in, res_all, delta_all, last_all, res, delta, near_high, near_low,
                send_sems, recv_sems, own_sems):
    x_hi, x_lo, y, z, core = place()
    x = x_hi * 2 + x_lo
    kinds = {kind: Group(kind) for kind in ("row", "col", "x", "y", "z", "core")}
    gx, gy, gz, gc = (kinds[k] for k in ("x", "y", "z", "core"))
    greet([kinds["row"], kinds["col"], gx])
    next_sem = [0]
    started = []

    def send(group, source, target):
        base = next_sem[0]
        next_sem[0] += group.size - 1
        copies = send_all(group, source, target, lambda s: send_sems.at[base + s - 1], lambda s: recv_sems.at[base + s - 1])
        started.append(copies)
        return copies

    def piece(i):
        quarter, lanes = i // 2, i % 2
        return full.at[x_lo, x_hi, y, core, quarter // 2, pl.ds(pl.multiple_of((quarter % 2) * 16, 16), 16),
                       pl.ds(pl.multiple_of(lanes * 512, 512), 512)]

    own_chunk = pltpu.make_async_copy(chunk, piece(z), own_sems.at[0])
    own_chunk.start()
    along_z = send(gz, lambda i: chunk, lambda i, s: piece(i))
    own_inverse = pltpu.make_async_copy(inverse.at[kinds["row"].me], inverse_in.at[kinds["row"].me], own_sems.at[1])
    own_inverse.start()
    own_wanted = pltpu.make_async_copy(wanted.at[kinds["row"].me], wanted_in.at[kinds["row"].me], own_sems.at[2])
    own_wanted.start()
    own_chunk.wait()
    arrived(along_z)
    x_first = send(gx, lambda i: full.at[x_lo, x_hi, y, core, 0], lambda i, s: full.at[i % 2, i // 2, y, core, 0])
    y_first = send(gy, lambda i: full.at[x_lo, x_hi, y, core, 1], lambda i, s: full.at[x_lo, x_hi, i, core, 1])
    arrived(x_first)
    y_last = send(gy, lambda i: full.at[:, :, y, core, 0], lambda i, s: full.at[:, :, i, core, 0])
    arrived(y_first)
    x_last = send(gx, lambda i: full.at[x_lo, x_hi, :, core, 1], lambda i, s: full.at[i % 2, i // 2, :, core, 1])
    inverse_sent = send(kinds["row"], lambda i: inverse.at[i], lambda i, s: inverse_in.at[i])
    wanted_sent = send(kinds["row"], lambda i: wanted.at[i], lambda i, s: wanted_in.at[i])
    arrived(y_last)
    across_0 = send(gc, lambda i: full.at[:, :, :, core, 0], lambda i, s: full.at[:, :, :, i, 0])
    arrived(x_last)
    across_1 = send(gc, lambda i: full.at[:, :, :, core, 1], lambda i, s: full.at[:, :, :, i, 1])

    def products(for_core, hi, pair, target):
        rows = jnp.concatenate([
            full[block, hi, pair * 2 + t, for_core].reshape(64, 1024) for t in range(2) for block in range(2)
        ], axis=0)
        inner = lax.dot_general(rows, points[...], NT, **DOTS)
        distance = squares_of(rows) + squares_row[0:1, :] - 2.0 * inner
        high, low = halves(jnp.exp(-distance * (0.5 / 1024)))
        tile[:, 0:384] = high
        tile[:, 384:768] = high
        tile[:, 768:1152] = low
        for part in range(2):
            span = slice(part * 512, part * 512 + 512)
            result = lax.dot_general(weights[span, :], tile[...], NT, **DOTS)
            target[hi, pair * 2, span, :] = result[:, 0:128]
            target[hi, pair * 2 + 1, span, :] = result[:, 128:256]

    def own_tile(i, carry):
        products(core, i // 2, i % 2, mine)
        return carry

    lax.fori_loop(0, 4, own_tile, 0)
    arrived(across_0)
    arrived(across_1)
    crossing_base = next_sem[0]
    next_sem[0] += 4
    other = (gc.at(gc.after(1)))

    def crossing(i):
        span = pl.ds(pl.multiple_of((i % 2) * 2, 2), 2)
        return pltpu.make_async_remote_copy(
            src_ref=theirs.at[i // 2, span], dst_ref=core_in.at[i // 2, span], send_sem=send_sems.at[crossing_base + i],
            recv_sem=recv_sems.at[crossing_base + i], device_id=other, device_id_type=MESH)

    def other_tile(i, carry):
        products(1 - core, i // 2, i % 2, theirs)
        crossing(i).start()
        return carry

    lax.fori_loop(0, 4, other_tile, 0)

    own_inverse.wait()
    arrived(inverse_sent)
    my_owner = jnp.where(x_lo == 0, owner[0], owner[1])
    inverse_all[kinds["row"].me] = inverse_in[my_owner]
    inverse_spread = send(kinds["row"], lambda i: inverse_all.at[kinds["row"].me], lambda i, s: inverse_all.at[i])

    def join(i, carry):
        crossing(i).wait_recv()
        for t in range(2):
            at = (i // 2, (i % 2) * 2 + t)
            mine[at] += core_in[at]
        return carry

    lax.fori_loop(0, 4, join, 0)

    def part(to_x, to_y, half):
        start = pl.multiple_of(((to_x % 2) * 2 + half) * 256, 256)
        return lambda: mine[to_x // 2, to_y, pl.ds(start, 256), :]

    for step in range(1, 4):
        code([part(gx.after(step), t, 0) for t in range(4)], x_out.at[step - 1])
    x_first = send(gx, lambda i: x_out.at[lax.rem(i + 3 - x, 4)], lambda i, s: x_in.at[s - 1])
    for step in range(1, 4):
        code([part(t, gy.after(step), 1) for t in range(4)], y_out.at[step - 1])
    y_first = send(gy, lambda i: y_out.at[lax.rem(i + 3 - y, 4)], lambda i, s: y_in.at[s - 1])

    first = full[0].reshape(1024, 1024)
    lengths = [
        jnp.transpose(jnp.broadcast_to(squares_of(full[0, t // 4, t % 4].reshape(128, 1024)), (128, 128)))[0:1, :]
        for t in range(8)
    ]
    lengths = jnp.concatenate(lengths, axis=1)
    for t in range(4):
        rows = full[1, t // 2, (t % 2) * 2:(t % 2) * 2 + 2].reshape(256, 1024)
        inner = lax.dot_general(rows, first, NT, **DOTS)
        high, low = halves(jnp.exp(-(squares_of(rows) + lengths - 2.0 * inner) * (0.5 / 1024)))
        near_high[t * 256:t * 256 + 256, :] = high
        near_low[t * 256:t * 256 + 256, :] = low

    arrived(x_first)
    for t in range(4):
        value = part(x, t, 0)()
        for i in range(3):
            value += wide(x_in[i, t * 256:t * 256 + 256, :]) * scale_of(x_in.at[i], 1024)
        u[t] = value
    for step in range(1, 4):
        code([lambda: u[gy.after(step)]], y_out_2.at[step - 1])
    y_last = send(gy, lambda i: y_out_2.at[lax.rem(i + 3 - y, 4)], lambda i, s: y_in_2.at[s - 1])
    arrived(y_first)
    for t in range(4):
        value = part(t, y, 1)()
        for i in range(3):
            value += wide(y_in[i, t * 256:t * 256 + 256, :]) * scale_of(y_in.at[i], 1024)
        v[t] = value
    for step in range(1, 4):
        code([lambda: v[gx.after(step)]], x_out_2.at[step - 1])
    x_last = send(gx, lambda i: x_out_2.at[lax.rem(i + 3 - x, 4)], lambda i, s: x_in_2.at[s - 1])
    arrived(y_last)
    value = u[y]
    for i in range(3):
        value += decode(y_in_2.at[i], 256)
    z_sum[0:256, :] = value
    arrived(x_last)
    value = v[x]
    for i in range(3):
        value += decode(x_in_2.at[i], 256)
    z_sum[256:512, :] = value

    def slab(i):
        return z_sum[pl.ds(pl.multiple_of(i * 64, 64), 64), :]

    for step in range(1, 8):
        code([lambda: slab(gz.after(step))], z_out.at[step - 1])
    to_z = send(gz, lambda i: z_out.at[lax.rem(i + 7 - z, 8)], lambda i, s: z_in.at[s - 1])
    own_wanted.wait()
    arrived(wanted_sent)
    left = lax.broadcasted_iota(jnp.int32, (64, 128), 1) < 64
    goal = jnp.where(left, wanted_in[owner[0]], wanted_in[owner[1]])
    arrived(to_z)
    value = slab(z)
    for i in range(7):
        value += decode(z_in.at[i], 64)
    residual = goal - value

    def spread(group, slots, value):
        code([lambda: value], slots.at[group.me])
        return send(group, lambda i: slots.at[group.me], lambda i, s: slots.at[i])

    def flip(value):
        return pltpu.roll(value, 64, 1)

    copies = spread(kinds["col"], res_all, residual)
    arrived(inverse_spread)
    rows_here = inverse_all[...].reshape(128, 1024)
    arrived(copies)
    for t in range(8):
        even, odd = decode(res_all.at[2 * t], 64), decode(res_all.at[2 * t + 1], 64)
        res[0, :, t * 128:t * 128 + 128] = jnp.where(left, even, flip(odd))
        res[1, :, t * 128:t * 128 + 128] = jnp.where(left, flip(even), odd)
    change_1 = lax.dot_general(res[0], rows_here, NT, precision=lax.Precision.HIGHEST, **DOTS)
    copies = spread(kinds["col"], delta_all, change_1)
    arrived(copies)
    for t in range(8):
        even, odd = decode(delta_all.at[2 * t], 64), decode(delta_all.at[2 * t + 1], 64)
        delta[:, t * 128:t * 128 + 128] = jnp.where(left, even, flip(odd))
    high, low = halves(delta[...])
    both = lax.dot_general(jnp.concatenate([high, low], axis=0), near_high[...], NT, **DOTS)
    moved = both[0:64] + both[64:128] + lax.dot_general(high, near_low[...], NT, **DOTS)
    change_2 = lax.dot_general(res[1] - moved, rows_here, NT, precision=lax.Precision.HIGHEST, **DOTS)
    copies = spread(kinds["row"], last_all, jnp.where(left, change_1, change_2))
    arrived(copies)
    for t in range(8):
        value = jnp.concatenate([decode(last_all.at[2 * t], 64), decode(last_all.at[2 * t + 1], 64)], axis=0)
        out[:, t * 128:t * 128 + 128] = jnp.transpose(value)
    for copies in started:
        sent(copies)

    def leave(i, carry):
        crossing(i).wait_send()
        return carry

    lax.fori_loop(0, 4, leave, 0)


def main(owner, chunk, points, squares_row, weights, inverse, wanted, collective_id):
    i16, bf16 = jnp.int16, jnp.bfloat16
    return pl.pallas_call(
        main_kernel,
        out_shape=jax.ShapeDtypeStruct((128, 1024), F32),
        in_specs=[pl.BlockSpec(memory_space=pltpu.SMEM), VMEM, VMEM, VMEM, VMEM, ANY, ANY],
        out_specs=VMEM,
        scratch_shapes=[
            pltpu.VMEM((2, 2, 4, 2, 2, 32, 1024), bf16),
            pltpu.VMEM((256, 1152), bf16),
            pltpu.VMEM((2, 4, 1024, 128), F32),
            pltpu.VMEM((2, 4, 1024, 128), F32),
            pltpu.VMEM((2, 4, 1024, 128), F32),
            pltpu.VMEM((3, 1040, 128), i16),
            pltpu.VMEM((3, 1040, 128), i16),
            pltpu.VMEM((3, 1040, 128), i16),
            pltpu.VMEM((3, 1040, 128), i16),
            pltpu.VMEM((4, 256, 128), F32),
            pltpu.VMEM((4, 256, 128), F32),
            pltpu.VMEM((3, 272, 128), i16),
            pltpu.VMEM((3, 272, 128), i16),
            pltpu.VMEM((3, 272, 128), i16),
            pltpu.VMEM((3, 272, 128), i16),
            pltpu.VMEM((512, 128), F32),
            pltpu.VMEM((7, 80, 128), i16),
            pltpu.VMEM((7, 80, 128), i16),
            pltpu.VMEM((16, 8, 1024), F32),
            pltpu.VMEM((16, 8, 1024), F32),
            pltpu.VMEM((16, 64, 128), F32),
            pltpu.VMEM((16, 80, 128), i16),
            pltpu.VMEM((16, 80, 128), i16),
            pltpu.VMEM((16, 80, 128), i16),
            pltpu.VMEM((2, 64, 1024), F32),
            pltpu.VMEM((64, 1024), F32),
            pltpu.VMEM((1024, 1024), bf16),
            pltpu.VMEM((1024, 1024), bf16),
            DMA((144,)), DMA((144,)), DMA((3,)),
        ],
        compiler_params=pltpu.CompilerParams(collective_id=collective_id, has_side_effects=True, vmem_limit_bytes=56 * 2**20),
    )(owner, chunk, points, squares_row, weights, inverse, wanted)


def on_device(points, targets, coeffs, block_inverse, block_order):
    blocks_here, per_col, features = points.shape
    classes = targets.shape[2]
    my_row = lax.axis_index("row")
    x_lo = my_row // 8
    ids = [block_order[0], block_order[1]]
    local = [b % blocks_here for b in ids]
    owner = [b // blocks_here for b in ids]

    def pick(array, step):
        return lax.dynamic_index_in_dim(array, local[step], 0, keepdims=False)

    def both(array):
        return jnp.stack([pick(array, 0), pick(array, 1)])

    own_points = both(points).reshape(2, 4, 16, 2, 512).transpose(0, 1, 3, 2, 4).reshape(16, 16, 512)
    (offers,) = exchange([own_points], [("row", "each")], 0)
    my_owner = jnp.where(x_lo == 0, owner[0], owner[1])
    chunk = lax.dynamic_index_in_dim(offers, my_owner, 0, keepdims=False)
    inverse_offer = both(block_inverse).reshape(16, 8, 1024)
    need = both(targets).astype(F32) - ridge_weight * both(coeffs)
    need = jnp.pad(need, ((0, 0), (0, 0), (0, 1024 - classes)))
    wanted_offer = need.transpose(2, 0, 1).reshape(16, 64, 128)

    flat_points = points.reshape(blocks_here * per_col, features)
    flat_wide = flat_points.astype(F32)
    squares_row = jnp.broadcast_to(jnp.sum(flat_wide * flat_wide, axis=1)[None, :], (8, blocks_here * per_col))
    flat_coeffs = jnp.pad(coeffs.reshape(blocks_here * per_col, classes), ((0, 0), (0, 1024 - classes)))
    turned = flat_coeffs.T
    kept = lax.reduce_precision(turned, 8, 7)
    high, low = kept.astype(jnp.bfloat16), (turned - kept).astype(jnp.bfloat16)
    weights = jnp.concatenate([high, low, high], axis=1)
    deltas = main(jnp.stack(owner), chunk, flat_points, squares_row, weights, inverse_offer, wanted_offer, 1)
    deltas = deltas.reshape(2, 64, 1024)[:, :, :classes]

    current = coeffs
    for step in range(2):
        before = lax.dynamic_index_in_dim(current, local[step], 0, keepdims=False)
        updated = jnp.where(my_row == owner[step], before + deltas[step], before)
        current = lax.dynamic_update_index_in_dim(current, updated, local[step], 0)
    return current


def solution(mesh):
    placed = (
        P("row", "col", None),
        P("row", "col", None),
        P("row", "col", None),
        P("row", "col", None),
        P(),
    )
    return jax.shard_map(
        on_device, mesh=mesh, in_specs=placed, out_specs=P("row", "col", None), check_vma=False
    )
```

time: 229 us -> 153 us (0.67)
  Pallas kernels: 161 us -> 132 us
  matrix products: 28.7 us -> 0 us
  local copies, waits for them, and re-layouts: 29.2 us -> 10.3 us
    pallas_call x4 -> x1, Pallas kernels: 66.5 us -> 15.7 us  [exchange(): pl.pallas_call(functools.partial(exchange_kernel, tuple(plan)), out_shape...]
    dot_general x6 -> x0, matrix products: 28.7 us -> none  [the longest x4 18 us: product(): lax.dot_general(left, right, (contract, ((), ())), precision=lax.Precisio...]
    pallas_call x2 -> x1, Pallas kernels: 94.3 us -> 116 us  [main(): pl.pallas_call(main_kernel, out_shape=jax.ShapeDtypeStruct((128, 1024), F...]
    reshape x6 -> x1, local copies, waits for them, and re-layouts: 8.7 us -> 0.46 us  [on_device(): coeffs.reshape(blocks_here * per_col, classes)]
    unnamed x15 -> x7, local copies, waits for them, and re-layouts: 6.02 us -> 2.64 us
    slice x5 -> x0, local copies, waits for them, and re-layouts: 3.26 us -> none  [the longest x3 3.11 us: on_device(): between = kern(ordered[1], ordered[0])]
where the time goes in v2:
time: 153 us
  Pallas kernels  132 us (86%)
  local copies, waits for them, and re-layouts  10.3 us (7%)
  other arithmetic  6.35 us (4%)
  between operations  4.21 us (3%)
    pallas_call x1, Pallas kernels, main(): pl.pallas_call(main_kernel, out_shape=jax.ShapeDtypeStruct((128, 1024), F...  116 us
    pallas_call x1, Pallas kernels, exchange(): pl.pallas_call(functools.partial(exchange_kernel, tuple(plan)), out_shape...  15.7 us

profile of v2, /device:TPU:1, one launch (start us, length us, event | category | flops | bytes accessed | tf_op | source)
XLA Modules:
  0.0 152.8 jit_solution(1297119339690236850)
XLA Ops:
  0.0 1.5 copy.15
  1.5 0.6 fusion.3
  6.2 0.6 pad_add_fusion.owner
  6.8 0.2 reshape.38
  7.0 0.7 copy.9
  7.7 15.7 %shard_map.55 = bf16[16,16,512]{2,1,0:T(8,128)(2,1)} custom-call(bf16[16,16,512]{2,1,0:T(8,128)(2,1)} %bitcast.29), custom_call_target="tpu_custom_call" | custom-call | tf_op jit(solution)/shard_map/pallas_call | solution.py:112
  23.4 1.3 dynamic-slice_bitcast_fusion.chunk
  24.8 0.2 multiply_reduce_fusion
  25.0 0.1 broadcast_in_dim.11
  25.1 0.6 broadcast_in_dim.12.squares_row
  25.7 0.5 copy.10
  26.1 0.2 fusion
  26.4 1.6 %pad_maximum_fusion.weights = bf16[1024,1152]{1,0:T(8,128)(2,1)} fusion(bf16[1024,384]{1,0:T(8,128)(2,1)S(1)} %get-tuple-element.10, bf16[1024,384]{1,0:T(8,128)(2,1)S(1)} %get-tuple-element.9), kind=kLoop, calls=%fused_computation | loop fusion | flops 7077888 | bytes 3932160 | tf_op jit(solution)/shard_map/concatenate | solution.py:451
  28.0 1.1 constant_dynamic-slice_fusion.4
  29.1 0.8 pad_maximum_fusion.1
  29.9 1.0 constant_dynamic-slice_fusion.2
  30.9 0.1 maximum_subtract_fusion
  31.0 0.3 reshape.43
  31.3 1.2 copy.11.wanted
  32.5 116.3 %shard_map.56 = f32[128,1024]{1,0:T(8,128)} custom-call(s32[2]{0:T(128)} %pad_add_fusion.owner, bf16[16,512]{1,0:T(8,128)(2,1)} %dynamic-slice_bitcast_fusion.chunk, bf16[384,1024]{1,0:T(8,128)(2,1)} %bitcast.25, f32[8,384]{1,0:T(8,128)} %broadcast_in_dim.12.squares_row, bf16[1024,1152]{1,0:T(8,128)(2,1)} %pad_maximum_fusion.weights, ...), custom_call_target="tpu_custom_call" | custom-call | tf_op jit(solution)/shard_map/pallas_call | solution.py:380
  148.9 1.0 fusion.1
  149.9 0.0 copy-start
  149.9 1.1 copy-done
  151.1 1.8 %fusion.2 = f32[6,64,1000]{2,1,0:T(8,128)} fusion(f32[6,64,1000]{2,1,0:T(8,128)} %copy-done, s32[]{:T(128)S(6)} %select_n.71, f32[2,64,1024]{2,1,0:T(8,128)} %bitcast.28, pred[]{:T(512)S(6)} %eq.14), kind=kLoop, calls=%fused_computation.11 | loop fusion | flops 128000 | bytes 786437 | tf_op jit(solution)/shard_map/jit(dynamic_update_index_in_dim)/dynamic_update_slice | solution.py:459
  (8 shorter events, 0.1 us)
Async XLA Ops:
  0.0 6.8 %copy-start.1 = (bf16[6,64,1024]{2,1,0:T(8,128)(2,1)S(1)}, bf16[6,64,1024]{2,1,0:T(8,128)(2,1)}, u32[]{:S(2)}) copy-start(bf16[6,64,1024]{2,1,0:T(8,128)(2,1)} %param.5) | copy-start | bytes 2359300
  0.0 1.5 copy-start.2
  149.9 1.1 copy-start

commit v3 on v2

--- a/solution.py
+++ b/solution.py
@@ -76,47 +76,6 @@
 def sent(copies):
     for out, _ in copies:
         out.wait_send()
-
-
-def exchange_start(group, mode, source, target, send_sems, recv_sems, own_sem):
-    pick = (lambda i: source.at[i]) if mode == "each" else (lambda i: source)
-    own = pltpu.make_async_copy(pick(group.me), target.at[group.me], own_sem)
-    own.start()
-    copies = send_all(group, pick, lambda i, step: target.at[i], lambda s: send_sems.at[s - 1], lambda s: recv_sems.at[s - 1])
-    return own, copies
-
-
-def exchange_wait(handle):
-    own, copies = handle
-    own.wait()
-    arrived(copies)
-    sent(copies)
-
-
-def exchange_kernel(plan, *refs):
-    count = len(plan)
-    sources, targets = refs[:count], refs[count:2 * count]
-    send_sems, recv_sems, own_sems = refs[2 * count:]
-    groups = {kind: Group(kind) for kind, _ in plan}
-    greet(list(groups.values()))
-    handles = [
-        exchange_start(groups[kind], mode, sources[i], targets[i], send_sems.at[i], recv_sems.at[i], own_sems.at[i])
-        for i, (kind, mode) in enumerate(plan)
-    ]
-    for handle in handles:
-        exchange_wait(handle)
-
-
-def exchange(arrays, plan, collective_id):
-    shapes = [a.shape if mode == "each" else (16, *a.shape) for a, (_, mode) in zip(arrays, plan)]
-    return pl.pallas_call(
-        functools.partial(exchange_kernel, tuple(plan)),
-        out_shape=[jax.ShapeDtypeStruct(s, a.dtype) for s, a in zip(shapes, arrays)],
-        in_specs=[ANY] * len(arrays),
-        out_specs=[ANY] * len(arrays),
-        scratch_shapes=[DMA((len(arrays), 15)), DMA((len(arrays), 15)), DMA((len(arrays),))],
-        compiler_params=pltpu.CompilerParams(collective_id=collective_id, has_side_effects=True),
-    )(*arrays)
 
 
 F32 = jnp.float32
@@ -165,37 +124,60 @@
     return high, (value - high.astype(F32)).astype(jnp.bfloat16)
 
 
-def main_kernel(owner, chunk, points, squares_row, weights, inverse, wanted, out,
-                full, tile, mine, theirs, core_in, x_out, x_in, y_out, y_in, u, v, y_out_2, y_in_2, x_out_2, x_in_2, z_sum,
-                z_out, z_in, inverse_in, inverse_all, wanted_in, res_all, delta_all, last_all, res, delta, near_high, near_low,
-                send_sems, recv_sems, own_sems):
+def turn(block):
+    return jnp.transpose(block)
+
+
+def main_kernel(owner, offers, points, coeffs, inverse, need, out,
+                offers_in, chunk, full, weights, squares_row, tile, mine, theirs, core_in, x_out, x_in, y_out, y_in, u, v,
+                y_out_2, y_in_2, x_out_2, x_in_2, z_sum, z_out, z_in, inverse_in, inverse_all, wanted, wanted_in, res_all,
+                delta_all, last_all, res, delta, near_high, near_low, send_sems, recv_sems, own_sems):
     x_hi, x_lo, y, z, core = place()
     x = x_hi * 2 + x_lo
     kinds = {kind: Group(kind) for kind in ("row", "col", "x", "y", "z", "core")}
-    gx, gy, gz, gc = (kinds[k] for k in ("x", "y", "z", "core"))
-    greet([kinds["row"], kinds["col"], gx])
+    gx, gy, gz, gc, gr = (kinds[k] for k in ("x", "y", "z", "core", "row"))
+    greet([gr, kinds["col"], gx])
     next_sem = [0]
     started = []
 
+    def take(count):
+        next_sem[0] += count
+        return next_sem[0] - count
+
     def send(group, source, target):
-        base = next_sem[0]
-        next_sem[0] += group.size - 1
+        base = take(group.size - 1)
         copies = send_all(group, source, target, lambda s: send_sems.at[base + s - 1], lambda s: recv_sems.at[base + s - 1])
         started.append(copies)
         return copies
+
+    own_offer = pltpu.make_async_copy(offers.at[gr.me], offers_in.at[gr.me], own_sems.at[0])
+    own_offer.start()
+    offered = send(gr, lambda i: offers.at[i], lambda i, s: offers_in.at[i])
+    for a in range(3):
+        span = slice(a * 128, a * 128 + 128)
+        squares_row[:, span] = turn(jnp.broadcast_to(squares_of(points[span, :]), (128, 128)))[0:8]
+        for b in range(8):
+            high, low = halves(turn(coeffs[span, b * 128:b * 128 + 128]))
+            weights[b * 128:b * 128 + 128, a * 128:a * 128 + 128] = high
+            weights[b * 128:b * 128 + 128, a * 128 + 384:a * 128 + 512] = low
+            weights[b * 128:b * 128 + 128, a * 128 + 768:a * 128 + 896] = high
+    for b in range(8):
+        block = turn(need[:, :, b * 128:b * 128 + 128].reshape(128, 128))
+        wanted[2 * b] = block[0:64]
+        wanted[2 * b + 1] = block[64:128]
+    own_offer.wait()
+    arrived(offered)
+    my_owner = jnp.where(x_lo == 0, owner[0], owner[1])
+    chunk[...] = offers_in[my_owner]
 
     def piece(i):
         quarter, lanes = i // 2, i % 2
         return full.at[x_lo, x_hi, y, core, quarter // 2, pl.ds(pl.multiple_of((quarter % 2) * 16, 16), 16),
                        pl.ds(pl.multiple_of(lanes * 512, 512), 512)]
 
-    own_chunk = pltpu.make_async_copy(chunk, piece(z), own_sems.at[0])
+    own_chunk = pltpu.make_async_copy(chunk, piece(z), own_sems.at[3])
     own_chunk.start()
     along_z = send(gz, lambda i: chunk, lambda i, s: piece(i))
-    own_inverse = pltpu.make_async_copy(inverse.at[kinds["row"].me], inverse_in.at[kinds["row"].me], own_sems.at[1])
-    own_inverse.start()
-    own_wanted = pltpu.make_async_copy(wanted.at[kinds["row"].me], wanted_in.at[kinds["row"].me], own_sems.at[2])
-    own_wanted.start()
     own_chunk.wait()
     arrived(along_z)
     x_first = send(gx, lambda i: full.at[x_lo, x_hi, y, core, 0], lambda i, s: full.at[i % 2, i // 2, y, core, 0])
@@ -204,78 +186,100 @@
     y_last = send(gy, lambda i: full.at[:, :, y, core, 0], lambda i, s: full.at[:, :, i, core, 0])
     arrived(y_first)
     x_last = send(gx, lambda i: full.at[x_lo, x_hi, :, core, 1], lambda i, s: full.at[i % 2, i // 2, :, core, 1])
-    inverse_sent = send(kinds["row"], lambda i: inverse.at[i], lambda i, s: inverse_in.at[i])
-    wanted_sent = send(kinds["row"], lambda i: wanted.at[i], lambda i, s: wanted_in.at[i])
     arrived(y_last)
     across_0 = send(gc, lambda i: full.at[:, :, :, core, 0], lambda i, s: full.at[:, :, :, i, 0])
     arrived(x_last)
     across_1 = send(gc, lambda i: full.at[:, :, :, core, 1], lambda i, s: full.at[:, :, :, i, 1])
 
-    def products(for_core, hi, pair, target):
+    own_inverse = pltpu.make_async_copy(inverse.at[gr.me], inverse_in.at[gr.me], own_sems.at[1])
+    own_inverse.start()
+    own_wanted = pltpu.make_async_copy(wanted.at[gr.me], wanted_in.at[gr.me], own_sems.at[2])
+    own_wanted.start()
+    inverse_sent = send(gr, lambda i: inverse.at[i], lambda i, s: inverse_in.at[i])
+    wanted_sent = send(gr, lambda i: wanted.at[i], lambda i, s: wanted_in.at[i])
+
+    def near(for_core, i):
         rows = jnp.concatenate([
-            full[block, hi, pair * 2 + t, for_core].reshape(64, 1024) for t in range(2) for block in range(2)
+            full[block, i // 2, (i % 2) * 2 + t, for_core].reshape(64, 1024) for t in range(2) for block in range(2)
         ], axis=0)
         inner = lax.dot_general(rows, points[...], NT, **DOTS)
         distance = squares_of(rows) + squares_row[0:1, :] - 2.0 * inner
         high, low = halves(jnp.exp(-distance * (0.5 / 1024)))
-        tile[:, 0:384] = high
-        tile[:, 384:768] = high
-        tile[:, 768:1152] = low
-        for part in range(2):
-            span = slice(part * 512, part * 512 + 512)
-            result = lax.dot_general(weights[span, :], tile[...], NT, **DOTS)
-            target[hi, pair * 2, span, :] = result[:, 0:128]
-            target[hi, pair * 2 + 1, span, :] = result[:, 128:256]
+        tile[for_core, i, :, 0:384] = high
+        tile[for_core, i, :, 384:768] = high
+        tile[for_core, i, :, 768:1152] = low
 
     def own_tile(i, carry):
-        products(core, i // 2, i % 2, mine)
+        near(core, i)
+        return carry
+
+    def other_tile(i, carry):
+        near(1 - core, i)
         return carry
 
     lax.fori_loop(0, 4, own_tile, 0)
     arrived(across_0)
     arrived(across_1)
-    crossing_base = next_sem[0]
-    next_sem[0] += 4
-    other = (gc.at(gc.after(1)))
-
-    def crossing(i):
-        span = pl.ds(pl.multiple_of((i % 2) * 2, 2), 2)
+    lax.fori_loop(0, 4, other_tile, 0)
+
+    crossing_base = take(4)
+    x_base, y_base = take(3), take(6)
+
+    def crossing(quarter):
         return pltpu.make_async_remote_copy(
-            src_ref=theirs.at[i // 2, span], dst_ref=core_in.at[i // 2, span], send_sem=send_sems.at[crossing_base + i],
-            recv_sem=recv_sems.at[crossing_base + i], device_id=other, device_id_type=MESH)
-
-    def other_tile(i, carry):
-        products(1 - core, i // 2, i % 2, theirs)
-        crossing(i).start()
-        return carry
-
-    lax.fori_loop(0, 4, other_tile, 0)
+            src_ref=theirs.at[quarter], dst_ref=core_in.at[quarter], send_sem=send_sems.at[crossing_base + quarter],
+            recv_sem=recv_sems.at[crossing_base + quarter], device_id=gc.at(gc.after(1)), device_id_type=MESH)
+
+    def products(for_core, quarter, target):
+        part = weights[quarter * 256:quarter * 256 + 256, :]
+        result = lax.dot_general(part, tile[for_core].reshape(1024, 1152), NT, **DOTS)
+        for i in range(8):
+            target[quarter, i // 4, i % 4] = result[:, i * 128:i * 128 + 128]
+
+    def summed(quarter, to_hi, to_y):
+        return lambda: mine[quarter, to_hi, to_y] + core_in[quarter, to_hi, to_y]
+
+    def x_copy(to, slot):
+        return pltpu.make_async_remote_copy(
+            src_ref=x_out.at[slot], dst_ref=x_in.at[slot], send_sem=send_sems.at[x_base + slot],
+            recv_sem=recv_sems.at[x_base + slot], device_id=gx.at(to), device_id_type=MESH)
+
+    def y_copy(step, low):
+        return pltpu.make_async_remote_copy(
+            src_ref=y_out.at[step - 1, low], dst_ref=y_in.at[step - 1, low],
+            send_sem=send_sems.at[y_base + 2 * (step - 1) + low], recv_sem=recv_sems.at[y_base + 2 * (step - 1) + low],
+            device_id=gy.at(gy.after(step)), device_id_type=MESH)
+
+    def leave_quarter(quarter):
+        low, half = quarter // 2, quarter % 2
+        crossing(quarter).wait_recv()
+        if half == 0:
+            for high in range(2):
+                to = high * 2 + low
+
+                @pl.when(to != x)
+                def _(high=high, to=to):
+                    slot = lax.rem(to + 3 - x, 4)
+                    code([summed(quarter, high, t) for t in range(4)], x_out.at[slot])
+                    x_copy(to, slot).start()
+        else:
+            for step in range(1, 4):
+                code([summed(quarter, t, gy.after(step)) for t in range(2)], y_out.at[step - 1, low])
+                y_copy(step, low).start()
+
+    order = (0, 1, 2, 3)
+    for place_in, quarter in enumerate(order):
+        products(1 - core, quarter, theirs)
+        crossing(quarter).start()
+        products(core, quarter, mine)
+        if place_in:
+            leave_quarter(order[place_in - 1])
+    leave_quarter(order[3])
 
     own_inverse.wait()
     arrived(inverse_sent)
-    my_owner = jnp.where(x_lo == 0, owner[0], owner[1])
-    inverse_all[kinds["row"].me] = inverse_in[my_owner]
-    inverse_spread = send(kinds["row"], lambda i: inverse_all.at[kinds["row"].me], lambda i, s: inverse_all.at[i])
-
-    def join(i, carry):
-        crossing(i).wait_recv()
-        for t in range(2):
-            at = (i // 2, (i % 2) * 2 + t)
-            mine[at] += core_in[at]
-        return carry
-
-    lax.fori_loop(0, 4, join, 0)
-
-    def part(to_x, to_y, half):
-        start = pl.multiple_of(((to_x % 2) * 2 + half) * 256, 256)
-        return lambda: mine[to_x // 2, to_y, pl.ds(start, 256), :]
-
-    for step in range(1, 4):
-        code([part(gx.after(step), t, 0) for t in range(4)], x_out.at[step - 1])
-    x_first = send(gx, lambda i: x_out.at[lax.rem(i + 3 - x, 4)], lambda i, s: x_in.at[s - 1])
-    for step in range(1, 4):
-        code([part(t, gy.after(step), 1) for t in range(4)], y_out.at[step - 1])
-    y_first = send(gy, lambda i: y_out.at[lax.rem(i + 3 - y, 4)], lambda i, s: y_in.at[s - 1])
+    inverse_all[gr.me] = inverse_in[my_owner]
+    inverse_spread = send(gr, lambda i: inverse_all.at[gr.me], lambda i, s: inverse_all.at[i])
 
     first = full[0].reshape(1024, 1024)
     lengths = [
@@ -290,20 +294,24 @@
         near_high[t * 256:t * 256 + 256, :] = high
         near_low[t * 256:t * 256 + 256, :] = low
 
-    arrived(x_first)
+    for slot in range(3):
+        x_copy(gx.after(slot + 1), slot).wait_recv()
     for t in range(4):
-        value = part(x, t, 0)()
+        value = summed(2 * x_lo, x_hi, t)()
         for i in range(3):
             value += wide(x_in[i, t * 256:t * 256 + 256, :]) * scale_of(x_in.at[i], 1024)
         u[t] = value
     for step in range(1, 4):
         code([lambda: u[gy.after(step)]], y_out_2.at[step - 1])
     y_last = send(gy, lambda i: y_out_2.at[lax.rem(i + 3 - y, 4)], lambda i, s: y_in_2.at[s - 1])
-    arrived(y_first)
+    for step in range(1, 4):
+        for low in range(2):
+            y_copy(step, low).wait_recv()
     for t in range(4):
-        value = part(t, y, 1)()
+        value = summed(2 * (t % 2) + 1, t // 2, y)()
         for i in range(3):
-            value += wide(y_in[i, t * 256:t * 256 + 256, :]) * scale_of(y_in.at[i], 1024)
+            slot = y_in.at[i, t % 2]
+            value += wide(y_in[i, t % 2, (t // 2) * 256:(t // 2) * 256 + 256, :]) * scale_of(slot, 512)
         v[t] = value
     for step in range(1, 4):
         code([lambda: v[gx.after(step)]], x_out_2.at[step - 1])
@@ -360,7 +368,7 @@
     both = lax.dot_general(jnp.concatenate([high, low], axis=0), near_high[...], NT, **DOTS)
     moved = both[0:64] + both[64:128] + lax.dot_general(high, near_low[...], NT, **DOTS)
     change_2 = lax.dot_general(res[1] - moved, rows_here, NT, precision=lax.Precision.HIGHEST, **DOTS)
-    copies = spread(kinds["row"], last_all, jnp.where(left, change_1, change_2))
+    copies = spread(gr, last_all, jnp.where(left, change_1, change_2))
     arrived(copies)
     for t in range(8):
         value = jnp.concatenate([decode(last_all.at[2 * t], 64), decode(last_all.at[2 * t + 1], 64)], axis=0)
@@ -368,30 +376,36 @@
     for copies in started:
         sent(copies)
 
-    def leave(i, carry):
-        crossing(i).wait_send()
-        return carry
-
-    lax.fori_loop(0, 4, leave, 0)
-
-
-def main(owner, chunk, points, squares_row, weights, inverse, wanted, collective_id):
+    for slot in range(3):
+        x_copy(gx.after(slot + 1), slot).wait_send()
+    for step in range(1, 4):
+        for low in range(2):
+            y_copy(step, low).wait_send()
+    for quarter in range(4):
+        crossing(quarter).wait_send()
+
+
+def main(owner, offers, points, coeffs, inverse, need, collective_id):
     i16, bf16 = jnp.int16, jnp.bfloat16
     return pl.pallas_call(
         main_kernel,
         out_shape=jax.ShapeDtypeStruct((128, 1024), F32),
-        in_specs=[pl.BlockSpec(memory_space=pltpu.SMEM), VMEM, VMEM, VMEM, VMEM, ANY, ANY],
+        in_specs=[pl.BlockSpec(memory_space=pltpu.SMEM), ANY, VMEM, VMEM, ANY, VMEM],
         out_specs=VMEM,
         scratch_shapes=[
+            pltpu.VMEM((16, 16, 512), bf16),
+            pltpu.VMEM((16, 512), bf16),
             pltpu.VMEM((2, 2, 4, 2, 2, 32, 1024), bf16),
-            pltpu.VMEM((256, 1152), bf16),
-            pltpu.VMEM((2, 4, 1024, 128), F32),
-            pltpu.VMEM((2, 4, 1024, 128), F32),
-            pltpu.VMEM((2, 4, 1024, 128), F32),
+            pltpu.VMEM((1024, 1152), bf16),
+            pltpu.VMEM((8, 384), F32),
+            pltpu.VMEM((2, 4, 256, 1152), bf16),
+            pltpu.VMEM((4, 2, 4, 256, 128), F32),
+            pltpu.VMEM((4, 2, 4, 256, 128), F32),
+            pltpu.VMEM((4, 2, 4, 256, 128), F32),
             pltpu.VMEM((3, 1040, 128), i16),
             pltpu.VMEM((3, 1040, 128), i16),
-            pltpu.VMEM((3, 1040, 128), i16),
-            pltpu.VMEM((3, 1040, 128), i16),
+            pltpu.VMEM((3, 2, 528, 128), i16),
+            pltpu.VMEM((3, 2, 528, 128), i16),
             pltpu.VMEM((4, 256, 128), F32),
             pltpu.VMEM((4, 256, 128), F32),
             pltpu.VMEM((3, 272, 128), i16),
@@ -404,6 +418,7 @@
             pltpu.VMEM((16, 8, 1024), F32),
             pltpu.VMEM((16, 8, 1024), F32),
             pltpu.VMEM((16, 64, 128), F32),
+            pltpu.VMEM((16, 64, 128), F32),
             pltpu.VMEM((16, 80, 128), i16),
             pltpu.VMEM((16, 80, 128), i16),
             pltpu.VMEM((16, 80, 128), i16),
@@ -411,17 +426,16 @@
             pltpu.VMEM((64, 1024), F32),
             pltpu.VMEM((1024, 1024), bf16),
             pltpu.VMEM((1024, 1024), bf16),
-            DMA((144,)), DMA((144,)), DMA((3,)),
+            DMA((160,)), DMA((160,)), DMA((4,)),
         ],
         compiler_params=pltpu.CompilerParams(collective_id=collective_id, has_side_effects=True, vmem_limit_bytes=56 * 2**20),
-    )(owner, chunk, points, squares_row, weights, inverse, wanted)
+    )(owner, offers, points, coeffs, inverse, need)
 
 
 def on_device(points, targets, coeffs, block_inverse, block_order):
     blocks_here, per_col, features = points.shape
     classes = targets.shape[2]
     my_row = lax.axis_index("row")
-    x_lo = my_row // 8
     ids = [block_order[0], block_order[1]]
     local = [b % blocks_here for b in ids]
     owner = [b // blocks_here for b in ids]
@@ -433,23 +447,13 @@
         return jnp.stack([pick(array, 0), pick(array, 1)])
 
     own_points = both(points).reshape(2, 4, 16, 2, 512).transpose(0, 1, 3, 2, 4).reshape(16, 16, 512)
-    (offers,) = exchange([own_points], [("row", "each")], 0)
-    my_owner = jnp.where(x_lo == 0, owner[0], owner[1])
-    chunk = lax.dynamic_index_in_dim(offers, my_owner, 0, keepdims=False)
     inverse_offer = both(block_inverse).reshape(16, 8, 1024)
     need = both(targets).astype(F32) - ridge_weight * both(coeffs)
     need = jnp.pad(need, ((0, 0), (0, 0), (0, 1024 - classes)))
-    wanted_offer = need.transpose(2, 0, 1).reshape(16, 64, 128)
 
     flat_points = points.reshape(blocks_here * per_col, features)
-    flat_wide = flat_points.astype(F32)
-    squares_row = jnp.broadcast_to(jnp.sum(flat_wide * flat_wide, axis=1)[None, :], (8, blocks_here * per_col))
     flat_coeffs = jnp.pad(coeffs.reshape(blocks_here * per_col, classes), ((0, 0), (0, 1024 - classes)))
-    turned = flat_coeffs.T
-    kept = lax.reduce_precision(turned, 8, 7)
-    high, low = kept.astype(jnp.bfloat16), (turned - kept).astype(jnp.bfloat16)
-    weights = jnp.concatenate([high, low, high], axis=1)
-    deltas = main(jnp.stack(owner), chunk, flat_points, squares_row, weights, inverse_offer, wanted_offer, 1)
+    deltas = main(jnp.stack(owner), own_points, flat_points, flat_coeffs, inverse_offer, need, 0)
     deltas = deltas.reshape(2, 64, 1024)[:, :, :classes]
 
     current = coeffs

time: 153 us -> 136 us (0.89)
  Pallas kernels: 132 us -> 118 us
  other arithmetic: 6.35 us -> 4.34 us
    pallas_call x1 -> x0, Pallas kernels: 15.7 us -> none  [exchange(): pl.pallas_call(functools.partial(exchange_kernel, tuple(plan)), out_shape...]
    pad x0 -> x2, local copies, waits for them, and re-layouts: none -> 2.16 us  [the longest x1 1.32 us: on_device(): jnp.pad(coeffs.reshape(blocks_here * per_col, classes), ((0, 0), (0, 1024...]
    reshape x3 -> x0, local copies, waits for them, and re-layouts: 1.96 us -> none  [the longest x2 1.5 us: on_device(): wanted_offer = need.transpose(2, 0, 1).reshape(16, 64, 128)]
    pallas_call x1, Pallas kernels: 116 us -> 118 us  [main(): pl.pallas_call(main_kernel, out_shape=jax.ShapeDtypeStruct((128, 1024), F...]
    concatenate x1 -> x0, other arithmetic: 1.61 us -> none  [on_device(): weights = jnp.concatenate([high, low, high], axis=1)]
where the time goes in v3:
time: 136 us; the launch traced here: 135 us
  Pallas kernels  118 us (87%)
  local copies, waits for them, and re-layouts  9.29 us (7%)
  other arithmetic  4.34 us (3%)
  between operations  3.75 us (3%)
    pallas_call x1, Pallas kernels, main(): pl.pallas_call(main_kernel, out_shape=jax.ShapeDtypeStruct((128, 1024), F...  118 us
    dynamic_slice x3, local copies, waits for them, and re-layouts, pick(): return lax.dynamic_index_in_dim(array, local[step], 0, keepdims=False)  3.04 us
    dynamic_update_slice x2, other arithmetic, on_device(): current = lax.dynamic_update_index_in_dim(current, updated, local[step], 0)  2.77 us

profile of v3, /device:TPU:1, one launch (start us, length us, event | category | flops | bytes accessed | tf_op | source)
XLA Modules:
  0.0 135.4 jit_solution(9206051955366613457)
XLA Ops:
  0.0 0.0 copy-start.1
  0.0 1.4 %copy.10 = f32[6,64,1000]{2,1,0:T(8,128)S(1)} copy(f32[6,64,1000]{2,1,0:T(8,128)} %param.7) | data formatting | bytes 3072000
  1.4 0.0 copy-done.1
  1.4 0.6 fusion.2
  5.7 0.7 pad_add_fusion.owner
  6.4 1.0 constant_dynamic-slice_fusion.2
  7.3 1.0 constant_dynamic-slice_fusion.6
  8.4 0.2 reshape.32
  8.6 0.7 copy.6
  9.3 1.1 constant_dynamic-slice_fusion.4
  10.4 0.8 pad_maximum_fusion
  11.2 0.1 maximum_subtract_fusion
  11.3 0.8 pad.9.need
  12.1 1.3 pad.8.coeffs
  13.5 118.0 %shard_map.55 = f32[128,1024]{1,0:T(8,128)} custom-call(s32[2]{0:T(128)} %pad_add_fusion.owner, bf16[16,16,512]{2,1,0:T(8,128)(2,1)} %bitcast.20, bf16[384,1024]{1,0:T(8,128)(2,1)} %bitcast.19, f32[384,1024]{1,0:T(8,128)} %pad.8.coeffs, f32[16,8,1024]{2,1,0:T(8,128)} %bitcast.16, f32[2,64,1024]{2,1,0:T(8,128)} %pad.9.need), custom_call_target="tpu_custom_call" | custom-call | tf_op jit(solution)/shard_map/pallas_call | solution.py:390
  131.5 1.0 fusion
  132.5 0.0 copy-start
  132.5 1.1 copy-done
  133.6 1.8 %fusion.1 = f32[6,64,1000]{2,1,0:T(8,128)} fusion(f32[6,64,1000]{2,1,0:T(8,128)} %copy-done, s32[]{:T(128)S(6)} %select_n.61, f32[2,64,1024]{2,1,0:T(8,128)} %bitcast.18, pred[]{:T(512)S(6)} %eq.10), kind=kLoop, calls=%fused_computation.5 | loop fusion | flops 128000 | bytes 786437 | tf_op jit(solution)/shard_map/jit(dynamic_update_index_in_dim)/dynamic_update_slice | solution.py:463
  (2 shorter events, 0.1 us)
Async XLA Ops:
  0.0 1.4 %copy-start.1 = (s32[96]{0:T(128)S(1)}, s32[96]{0:T(128)}, u32[]{:S(2)}) copy-start(s32[96]{0:T(128)} %param.9) | copy-start | bytes 1156
  132.5 1.1 copy-start

commit v4 on v3

--- a/solution.py
+++ b/solution.py
@@ -45,12 +45,15 @@
         return lax.rem(self.me + self.size - step, self.size)
 
 
-def greet(groups):
+def signal_all(groups):
     barrier = pltpu.get_barrier_semaphore()
     for group in groups:
         for step in range(1, group.size):
             pl.semaphore_signal(barrier, inc=1, device_id=group.at(group.after(step)), device_id_type=MESH)
-    pl.semaphore_wait(barrier, sum(group.size - 1 for group in groups))
+
+
+def wait_all(groups):
+    pl.semaphore_wait(pltpu.get_barrier_semaphore(), sum(group.size - 1 for group in groups))
 
 
 def send_all(group, source, target, send_sem, recv_sem):
@@ -80,6 +83,7 @@
 
 F32 = jnp.float32
 NT = (((1,), (1,)), ((), ()))
+NN = (((1,), (0,)), ((), ()))
 LIMIT = 32000.0
 DOTS = dict(preferred_element_type=jnp.float32)
 
@@ -125,18 +129,28 @@
 
 
 def turn(block):
+    rows, lanes = block.shape
+    if lanes < 128:
+        block = jnp.concatenate([block, jnp.zeros((rows, 128 - lanes), block.dtype)], axis=1)
     return jnp.transpose(block)
 
 
-def main_kernel(owner, offers, points, coeffs, inverse, need, out,
-                offers_in, chunk, full, weights, squares_row, tile, mine, theirs, core_in, x_out, x_in, y_out, y_in, u, v,
+def main_kernel(order, points, targets, coeffs, block_inverse, out,
+                offers, inverse, offers_in, chunk, full, weights, squares_row, tile, mine, apart, theirs, core_in, x_out, x_in, y_out, y_in, u, v,
                 y_out_2, y_in_2, x_out_2, x_in_2, z_sum, z_out, z_in, inverse_in, inverse_all, wanted, wanted_in, res_all,
-                delta_all, last_all, res, delta, near_high, near_low, send_sems, recv_sems, own_sems):
+                delta_all, last_all, res, delta, near_high, near_low, linked, send_sems, recv_sems, own_sems):
     x_hi, x_lo, y, z, core = place()
     x = x_hi * 2 + x_lo
+    classes = coeffs.shape[2]
+    blocks_here = points.shape[0]
+    owner, local = [order[t] // blocks_here for t in range(2)], [order[t] % blocks_here for t in range(2)]
     kinds = {kind: Group(kind) for kind in ("row", "col", "x", "y", "z", "core")}
     gx, gy, gz, gc, gr = (kinds[k] for k in ("x", "y", "z", "core", "row"))
-    greet([gr, kinds["col"], gx])
+    signal_all([gr, kinds["col"], gx])
+    for block in range(2):
+        for q in range(8):
+            offers[block * 8 + q] = points[local[block], (q // 2) * 16:(q // 2) * 16 + 16, (q % 2) * 512:(q % 2) * 512 + 512]
+    wait_all([gr, kinds["col"], gx])
     next_sem = [0]
     started = []
 
@@ -155,16 +169,21 @@
     offered = send(gr, lambda i: offers.at[i], lambda i, s: offers_in.at[i])
     for a in range(3):
         span = slice(a * 128, a * 128 + 128)
-        squares_row[:, span] = turn(jnp.broadcast_to(squares_of(points[span, :]), (128, 128)))[0:8]
+        squares_row[:, span] = turn(jnp.broadcast_to(squares_of(points[2 * a:2 * a + 2].reshape(128, 1024)), (128, 128)))[0:8]
         for b in range(8):
-            high, low = halves(turn(coeffs[span, b * 128:b * 128 + 128]))
+            high, low = halves(turn(coeffs[2 * a:2 * a + 2, :, b * 128:min(b * 128 + 128, classes)].reshape(128, -1)))
             weights[b * 128:b * 128 + 128, a * 128:a * 128 + 128] = high
             weights[b * 128:b * 128 + 128, a * 128 + 384:a * 128 + 512] = low
             weights[b * 128:b * 128 + 128, a * 128 + 768:a * 128 + 896] = high
     for b in range(8):
-        block = turn(need[:, :, b * 128:b * 128 + 128].reshape(128, 128))
-        wanted[2 * b] = block[0:64]
-        wanted[2 * b + 1] = block[64:128]
+        lanes = slice(b * 128, min(b * 128 + 128, classes))
+        block = turn(jnp.concatenate([
+            targets[local[t], :, lanes].astype(F32) - ridge_weight * coeffs[local[t], :, lanes] for t in range(2)
+        ], axis=0))
+        code([lambda: block[0:64]], wanted.at[2 * b])
+        code([lambda: block[64:128]], wanted.at[2 * b + 1])
+    for q in range(16):
+        inverse[q] = block_inverse[local[q // 8], (q % 8) * 8:(q % 8) * 8 + 8, :]
     own_offer.wait()
     arrived(offered)
     my_owner = jnp.where(x_lo == 0, owner[0], owner[1])
@@ -186,23 +205,19 @@
     y_last = send(gy, lambda i: full.at[:, :, y, core, 0], lambda i, s: full.at[:, :, i, core, 0])
     arrived(y_first)
     x_last = send(gx, lambda i: full.at[x_lo, x_hi, :, core, 1], lambda i, s: full.at[i % 2, i // 2, :, core, 1])
+    own_inverse = pltpu.make_async_copy(inverse.at[gr.me], inverse_in.at[gr.me], own_sems.at[1])
+    own_inverse.start()
+    inverse_sent = send(gr, lambda i: inverse.at[i], lambda i, s: inverse_in.at[i])
     arrived(y_last)
     across_0 = send(gc, lambda i: full.at[:, :, :, core, 0], lambda i, s: full.at[:, :, :, i, 0])
     arrived(x_last)
     across_1 = send(gc, lambda i: full.at[:, :, :, core, 1], lambda i, s: full.at[:, :, :, i, 1])
 
-    own_inverse = pltpu.make_async_copy(inverse.at[gr.me], inverse_in.at[gr.me], own_sems.at[1])
-    own_inverse.start()
-    own_wanted = pltpu.make_async_copy(wanted.at[gr.me], wanted_in.at[gr.me], own_sems.at[2])
-    own_wanted.start()
-    inverse_sent = send(gr, lambda i: inverse.at[i], lambda i, s: inverse_in.at[i])
-    wanted_sent = send(gr, lambda i: wanted.at[i], lambda i, s: wanted_in.at[i])
-
     def near(for_core, i):
         rows = jnp.concatenate([
             full[block, i // 2, (i % 2) * 2 + t, for_core].reshape(64, 1024) for t in range(2) for block in range(2)
         ], axis=0)
-        inner = lax.dot_general(rows, points[...], NT, **DOTS)
+        inner = lax.dot_general(rows, points[...].reshape(384, 1024), NT, **DOTS)
         distance = squares_of(rows) + squares_row[0:1, :] - 2.0 * inner
         high, low = halves(jnp.exp(-distance * (0.5 / 1024)))
         tile[for_core, i, :, 0:384] = high
@@ -218,6 +233,11 @@
         return carry
 
     lax.fori_loop(0, 4, own_tile, 0)
+    own_inverse.wait()
+    arrived(inverse_sent)
+    inverse_all[gr.me] = inverse_in[my_owner]
+    inverse_spread = send(gr, lambda i: inverse_all.at[gr.me], lambda i, s: inverse_all.at[i])
+    wanted_sent = send(gr, lambda i: wanted.at[i], lambda i, s: wanted_in.at[i])
     arrived(across_0)
     arrived(across_1)
     lax.fori_loop(0, 4, other_tile, 0)
@@ -230,14 +250,12 @@
             src_ref=theirs.at[quarter], dst_ref=core_in.at[quarter], send_sem=send_sems.at[crossing_base + quarter],
             recv_sem=recv_sems.at[crossing_base + quarter], device_id=gc.at(gc.after(1)), device_id_type=MESH)
 
-    def products(for_core, quarter, target):
+    def products(for_core, quarter):
         part = weights[quarter * 256:quarter * 256 + 256, :]
-        result = lax.dot_general(part, tile[for_core].reshape(1024, 1152), NT, **DOTS)
-        for i in range(8):
-            target[quarter, i // 4, i % 4] = result[:, i * 128:i * 128 + 128]
+        return lax.dot_general(part, tile[for_core].reshape(1024, 1152), NT, **DOTS)
 
     def summed(quarter, to_hi, to_y):
-        return lambda: mine[quarter, to_hi, to_y] + core_in[quarter, to_hi, to_y]
+        return lambda: mine[quarter, to_hi, to_y]
 
     def x_copy(to, slot):
         return pltpu.make_async_remote_copy(
@@ -253,6 +271,9 @@
     def leave_quarter(quarter):
         low, half = quarter // 2, quarter % 2
         crossing(quarter).wait_recv()
+        factor = scale_of(core_in.at[quarter], 2048)
+        for i in range(8):
+            mine[quarter, i // 4, i % 4] += wide(core_in[quarter, i * 256:i * 256 + 256, :]) * factor
         if half == 0:
             for high in range(2):
                 to = high * 2 + low
@@ -267,32 +288,17 @@
                 code([summed(quarter, t, gy.after(step)) for t in range(2)], y_out.at[step - 1, low])
                 y_copy(step, low).start()
 
-    order = (0, 1, 2, 3)
-    for place_in, quarter in enumerate(order):
-        products(1 - core, quarter, theirs)
+    for quarter in range(4):
+        result = products(1 - core, quarter)
+        for i in range(8):
+            apart[i] = result[:, i * 128:i * 128 + 128]
+        code([lambda i=i: apart[i] for i in range(8)], theirs.at[quarter])
         crossing(quarter).start()
-        products(core, quarter, mine)
-        if place_in:
-            leave_quarter(order[place_in - 1])
-    leave_quarter(order[3])
-
-    own_inverse.wait()
-    arrived(inverse_sent)
-    inverse_all[gr.me] = inverse_in[my_owner]
-    inverse_spread = send(gr, lambda i: inverse_all.at[gr.me], lambda i, s: inverse_all.at[i])
-
-    first = full[0].reshape(1024, 1024)
-    lengths = [
-        jnp.transpose(jnp.broadcast_to(squares_of(full[0, t // 4, t % 4].reshape(128, 1024)), (128, 128)))[0:1, :]
-        for t in range(8)
-    ]
-    lengths = jnp.concatenate(lengths, axis=1)
-    for t in range(4):
-        rows = full[1, t // 2, (t % 2) * 2:(t % 2) * 2 + 2].reshape(256, 1024)
-        inner = lax.dot_general(rows, first, NT, **DOTS)
-        high, low = halves(jnp.exp(-(squares_of(rows) + lengths - 2.0 * inner) * (0.5 / 1024)))
-        near_high[t * 256:t * 256 + 256, :] = high
-        near_low[t * 256:t * 256 + 256, :] = low
+    for quarter in range(4):
+        result = products(core, quarter)
+        for i in range(8):
+            mine[quarter, i // 4, i % 4] = result[:, i * 128:i * 128 + 128]
+        leave_quarter(quarter)
 
     for slot in range(3):
         x_copy(gx.after(slot + 1), slot).wait_recv()
@@ -333,10 +339,23 @@
     for step in range(1, 8):
         code([lambda: slab(gz.after(step))], z_out.at[step - 1])
     to_z = send(gz, lambda i: z_out.at[lax.rem(i + 7 - z, 8)], lambda i, s: z_in.at[s - 1])
-    own_wanted.wait()
+    first = full[0].reshape(1024, 1024)
+    lengths = [
+        jnp.transpose(jnp.broadcast_to(squares_of(full[0, t // 4, t % 4].reshape(128, 1024)), (128, 128)))[0:1, :]
+        for t in range(8)
+    ]
+    lengths = jnp.concatenate(lengths, axis=1)
+    for t in range(4):
+        rows = full[1, t // 2, (t % 2) * 2:(t % 2) * 2 + 2].reshape(256, 1024)
+        inner = lax.dot_general(rows, first, NT, **DOTS)
+        high, low = halves(jnp.exp(-(squares_of(rows) + lengths - 2.0 * inner) * (0.5 / 1024)))
+        near_high[t * 256:t * 256 + 256, :] = high
+        near_low[t * 256:t * 256 + 256, :] = low
+
+    left = lax.broadcasted_iota(jnp.int32, (64, 128), 1) < 64
+    wanted_in[gr.me] = wanted[gr.me]
     arrived(wanted_sent)
-    left = lax.broadcasted_iota(jnp.int32, (64, 128), 1) < 64
-    goal = jnp.where(left, wanted_in[owner[0]], wanted_in[owner[1]])
+    goal = jnp.where(left, decode(wanted_in[owner[0]], 64), decode(wanted_in[owner[1]], 64))
     arrived(to_z)
     value = slab(z)
     for i in range(7):
@@ -353,6 +372,9 @@
     copies = spread(kinds["col"], res_all, residual)
     arrived(inverse_spread)
     rows_here = inverse_all[...].reshape(128, 1024)
+    high, low = halves(rows_here)
+    across = lax.dot_general(jnp.concatenate([high, low], axis=0), near_high[...], NN, **DOTS)
+    linked[...] = across[0:128] + across[128:256] + lax.dot_general(high, near_low[...], NN, **DOTS)
     arrived(copies)
     for t in range(8):
         even, odd = decode(res_all.at[2 * t], 64), decode(res_all.at[2 * t + 1], 64)
@@ -360,19 +382,18 @@
         res[1, :, t * 128:t * 128 + 128] = jnp.where(left, flip(even), odd)
     change_1 = lax.dot_general(res[0], rows_here, NT, precision=lax.Precision.HIGHEST, **DOTS)
     copies = spread(kinds["col"], delta_all, change_1)
+    change_2 = lax.dot_general(res[1], rows_here, NT, precision=lax.Precision.HIGHEST, **DOTS)
     arrived(copies)
     for t in range(8):
         even, odd = decode(delta_all.at[2 * t], 64), decode(delta_all.at[2 * t + 1], 64)
         delta[:, t * 128:t * 128 + 128] = jnp.where(left, even, flip(odd))
-    high, low = halves(delta[...])
-    both = lax.dot_general(jnp.concatenate([high, low], axis=0), near_high[...], NT, **DOTS)
-    moved = both[0:64] + both[64:128] + lax.dot_general(high, near_low[...], NT, **DOTS)
-    change_2 = lax.dot_general(res[1] - moved, rows_here, NT, precision=lax.Precision.HIGHEST, **DOTS)
+    change_2 -= lax.dot_general(delta[...], linked[...], NT, precision=lax.Precision.HIGHEST, **DOTS)
     copies = spread(gr, last_all, jnp.where(left, change_1, change_2))
     arrived(copies)
     for t in range(8):
         value = jnp.concatenate([decode(last_all.at[2 * t], 64), decode(last_all.at[2 * t + 1], 64)], axis=0)
-        out[:, t * 128:t * 128 + 128] = jnp.transpose(value)
+        lanes = min(128, classes - t * 128)
+        out[:, t * 128:t * 128 + lanes] = jnp.transpose(value)[:, 0:lanes]
     for copies in started:
         sent(copies)
 
@@ -385,14 +406,16 @@
         crossing(quarter).wait_send()
 
 
-def main(owner, offers, points, coeffs, inverse, need, collective_id):
+def main(order, points, targets, coeffs, block_inverse, collective_id):
     i16, bf16 = jnp.int16, jnp.bfloat16
     return pl.pallas_call(
         main_kernel,
-        out_shape=jax.ShapeDtypeStruct((128, 1024), F32),
-        in_specs=[pl.BlockSpec(memory_space=pltpu.SMEM), ANY, VMEM, VMEM, ANY, VMEM],
+        out_shape=jax.ShapeDtypeStruct((128, coeffs.shape[2]), F32),
+        in_specs=[pl.BlockSpec(memory_space=pltpu.SMEM), VMEM, VMEM, VMEM, VMEM],
         out_specs=VMEM,
         scratch_shapes=[
+            pltpu.VMEM((16, 16, 512), bf16),
+            pltpu.VMEM((16, 8, 1024), F32),
             pltpu.VMEM((16, 16, 512), bf16),
             pltpu.VMEM((16, 512), bf16),
             pltpu.VMEM((2, 2, 4, 2, 2, 32, 1024), bf16),
@@ -400,8 +423,9 @@
             pltpu.VMEM((8, 384), F32),
             pltpu.VMEM((2, 4, 256, 1152), bf16),
             pltpu.VMEM((4, 2, 4, 256, 128), F32),
-            pltpu.VMEM((4, 2, 4, 256, 128), F32),
-            pltpu.VMEM((4, 2, 4, 256, 128), F32),
+            pltpu.VMEM((8, 256, 128), F32),
+            pltpu.VMEM((4, 2064, 128), i16),
+            pltpu.VMEM((4, 2064, 128), i16),
             pltpu.VMEM((3, 1040, 128), i16),
             pltpu.VMEM((3, 1040, 128), i16),
             pltpu.VMEM((3, 2, 528, 128), i16),
@@ -417,8 +441,8 @@
             pltpu.VMEM((7, 80, 128), i16),
             pltpu.VMEM((16, 8, 1024), F32),
             pltpu.VMEM((16, 8, 1024), F32),
-            pltpu.VMEM((16, 64, 128), F32),
-            pltpu.VMEM((16, 64, 128), F32),
+            pltpu.VMEM((16, 80, 128), i16),
+            pltpu.VMEM((16, 80, 128), i16),
             pltpu.VMEM((16, 80, 128), i16),
             pltpu.VMEM((16, 80, 128), i16),
             pltpu.VMEM((16, 80, 128), i16),
@@ -426,41 +450,23 @@
             pltpu.VMEM((64, 1024), F32),
             pltpu.VMEM((1024, 1024), bf16),
             pltpu.VMEM((1024, 1024), bf16),
+            pltpu.VMEM((128, 1024), F32),
             DMA((160,)), DMA((160,)), DMA((4,)),
         ],
         compiler_params=pltpu.CompilerParams(collective_id=collective_id, has_side_effects=True, vmem_limit_bytes=56 * 2**20),
-    )(owner, offers, points, coeffs, inverse, need)
+    )(order, points, targets, coeffs, block_inverse)
 
 
 def on_device(points, targets, coeffs, block_inverse, block_order):
-    blocks_here, per_col, features = points.shape
+    blocks_here, per_col, _ = points.shape
     classes = targets.shape[2]
-    my_row = lax.axis_index("row")
-    ids = [block_order[0], block_order[1]]
-    local = [b % blocks_here for b in ids]
-    owner = [b // blocks_here for b in ids]
-
-    def pick(array, step):
-        return lax.dynamic_index_in_dim(array, local[step], 0, keepdims=False)
-
-    def both(array):
-        return jnp.stack([pick(array, 0), pick(array, 1)])
-
-    own_points = both(points).reshape(2, 4, 16, 2, 512).transpose(0, 1, 3, 2, 4).reshape(16, 16, 512)
-    inverse_offer = both(block_inverse).reshape(16, 8, 1024)
-    need = both(targets).astype(F32) - ridge_weight * both(coeffs)
-    need = jnp.pad(need, ((0, 0), (0, 0), (0, 1024 - classes)))
-
-    flat_points = points.reshape(blocks_here * per_col, features)
-    flat_coeffs = jnp.pad(coeffs.reshape(blocks_here * per_col, classes), ((0, 0), (0, 1024 - classes)))
-    deltas = main(jnp.stack(owner), own_points, flat_points, flat_coeffs, inverse_offer, need, 0)
-    deltas = deltas.reshape(2, 64, 1024)[:, :, :classes]
-
+    deltas = main(block_order, points, targets, coeffs, block_inverse, 0)
+    deltas = deltas.reshape(2, per_col, classes)
+
+    block = lax.axis_index("row") * blocks_here + lax.broadcasted_iota(jnp.int32, (blocks_here, 1, 1), 0)
     current = coeffs
     for step in range(2):
-        before = lax.dynamic_index_in_dim(current, local[step], 0, keepdims=False)
-        updated = jnp.where(my_row == owner[step], before + deltas[step], before)
-        current = lax.dynamic_update_index_in_dim(current, updated, local[step], 0)
+        current = jnp.where(block == block_order[step], current + deltas[step][None], current)
     return current
 
 

time: 136 us -> 123 us (0.904)
  local copies, waits for them, and re-layouts: 9.29 us -> 2.39 us
  between operations: 3.75 us -> 0.04 us
  other arithmetic: 4.34 us -> 2.82 us
    dynamic_slice x4 -> x0, local copies, waits for them, and re-layouts: 3.08 us -> none  [the longest x3 3.04 us: pick(): return lax.dynamic_index_in_dim(array, local[step], 0, keepdims=False)]
    dynamic_update_slice x2 -> x0, other arithmetic: 2.77 us -> none  [on_device(): current = lax.dynamic_update_index_in_dim(current, updated, local[step], 0)]
    unnamed x5 -> x2, local copies, waits for them, and re-layouts: 2.56 us -> 0.01 us
    pad x2 -> x0, local copies, waits for them, and re-layouts: 2.16 us -> none  [the longest x1 1.32 us: on_device(): jnp.pad(coeffs.reshape(blocks_here * per_col, classes), ((0, 0), (0, 1024...]
    slice x1 -> x2, local copies, waits for them, and re-layouts: 0.58 us -> 2.38 us  [the longest x1 1.31 us: on_device(): block_order[step]]
    select_n x0 -> x1, other arithmetic: none -> 1.56 us  [on_device(): jnp.where(block == block_order[step], current + deltas[step][None], current)]
    another operation x3 -> x0, other arithmetic: 1.51 us -> none  [the longest x2 0.86 us: both(): return jnp.stack([pick(array, 0), pick(array, 1)])]
where the time goes in v4:
time: 123 us; the launch traced here: 122 us
  Pallas kernels  117 us (95%)
  other arithmetic  2.82 us (2%)
  local copies, waits for them, and re-layouts  2.39 us (2%)
    pallas_call x1, Pallas kernels, main(): pl.pallas_call(main_kernel, out_shape=jax.ShapeDtypeStruct((128, coeffs.s...  117 us

profile of v4, /device:TPU:1, one launch (start us, length us, event | category | flops | bytes accessed | tf_op | source)
XLA Modules:
  0.0 122.4 jit_solution(12907215777678996489)
XLA Ops:
  0.0 1.3 %fusion.3 = (s32[1]{0:T(128)}, s32[1]{0:T(128)}) fusion(s32[96]{0:T(128)} %order.1), kind=kLoop, calls=%fused_computation.6 | loop fusion | bytes 16 | tf_op jit(solution)/shard_map/slice | solution.py:469
  1.3 1.3 %fusion = (pred[6]{0:T(512)(128)(4,1)S(1)}, pred[6]{0:T(512)(128)(4,1)S(1)}) fusion(s32[]{:T(128)} %bitcast.1, s32[]{:T(128)S(6)} %mul.3, s32[]{:T(128)} %bitcast), kind=kLoop, calls=%fused_computation.3 | loop fusion | flops 18 | bytes 24 | tf_op jit(solution)/shard_map/eq | solution.py:469
  2.6 0.0 copy-start
  2.6 117.1 %shard_map.55 = f32[128,1000]{1,0:T(8,128)} custom-call(s32[96]{0:T(128)} %order.1, bf16[6,64,1024]{2,1,0:T(8,128)(2,1)} %points.1, bf16[6,64,1000]{2,1,0:T(8,128)(2,1)} %targets.1, f32[6,64,1000]{2,1,0:T(8,128)} %coeffs.1, f32[6,64,1024]{2,1,0:T(8,128)} %block_inverse.1), custom_call_target="tpu_custom_call" | custom-call | tf_op jit(solution)/shard_map/pallas_call | solution.py:411
  119.7 1.1 fusion.2
  120.8 0.0 copy-done
  120.8 1.6 %add_select_fusion = f32[6,64,1000]{2,1,0:T(8,128)} fusion(f32[6,64,1000]{2,1,0:T(8,128)S(1)} %copy-done, f32[64,1000]{1,0:T(8,128)S(1)} %get-tuple-element.6, f32[64,1000]{1,0:T(8,128)S(1)} %get-tuple-element.5, pred[6]{0:T(512)(128)(4,1)S(1)} %get-tuple-element.9, pred[6]{0:T(512)(128)(4,1)S(1)} %get-tuple-element.10), kind=kLoop, calls=%fused_computation | loop fusion | flops 1536000 | bytes 3584012 | tf_op jit(solution)/shard_map/jit(_where)/select_n | solution.py:469
Async XLA Ops:
  2.6 118.2 %copy-start = (f32[6,64,1000]{2,1,0:T(8,128)S(1)}, f32[6,64,1000]{2,1,0:T(8,128)}, u32[]{:S(2)}) copy-start(f32[6,64,1000]{2,1,0:T(8,128)} %coeffs.1) | copy-start | bytes 4608004

commit v5 on v4

--- a/solution.py
+++ b/solution.py
@@ -135,10 +135,10 @@
     return jnp.transpose(block)
 
 
-def main_kernel(order, points, targets, coeffs, block_inverse, out,
-                offers, inverse, offers_in, chunk, full, weights, squares_row, tile, mine, apart, theirs, core_in, x_out, x_in, y_out, y_in, u, v,
+def main_kernel(order, points_in, targets_in, coeffs_in, block_inverse_in, out_1, out_2, hit,
+                points, targets, coeffs, block_inverse, offers, inverse, offers_in, chunk, full, weights, squares_row, tile, mine, apart, theirs, core_in, x_out, x_in, y_out, y_in, u, v,
                 y_out_2, y_in_2, x_out_2, x_in_2, z_sum, z_out, z_in, inverse_in, inverse_all, wanted, wanted_in, res_all,
-                delta_all, last_all, res, delta, near_high, near_low, linked, send_sems, recv_sems, own_sems):
+                delta_all, last_all, res, delta, near_high, near_low, linked, send_sems, recv_sems, own_sems, load_sems):
     x_hi, x_lo, y, z, core = place()
     x = x_hi * 2 + x_lo
     classes = coeffs.shape[2]
@@ -147,6 +147,17 @@
     kinds = {kind: Group(kind) for kind in ("row", "col", "x", "y", "z", "core")}
     gx, gy, gz, gc, gr = (kinds[k] for k in ("x", "y", "z", "core", "row"))
     signal_all([gr, kinds["col"], gx])
+    loads = [
+        pltpu.make_async_copy(source, target, load_sems.at[i]) for i, (source, target) in enumerate((
+            (points_in, points), (coeffs_in, coeffs), (targets_in, targets), (block_inverse_in, block_inverse)))
+    ]
+    for load in loads:
+        load.start()
+    for t in range(2):
+        for b in range(blocks_here):
+            here = jnp.where(gr.me * blocks_here + b == order[t], 1.0, 0.0)
+            hit[t * 8 + b:t * 8 + b + 1, :] = jnp.full((1, 128), here, F32)
+    loads[0].wait()
     for block in range(2):
         for q in range(8):
             offers[block * 8 + q] = points[local[block], (q // 2) * 16:(q // 2) * 16 + 16, (q % 2) * 512:(q % 2) * 512 + 512]
@@ -167,6 +178,7 @@
     own_offer = pltpu.make_async_copy(offers.at[gr.me], offers_in.at[gr.me], own_sems.at[0])
     own_offer.start()
     offered = send(gr, lambda i: offers.at[i], lambda i, s: offers_in.at[i])
+    loads[1].wait()
     for a in range(3):
         span = slice(a * 128, a * 128 + 128)
         squares_row[:, span] = turn(jnp.broadcast_to(squares_of(points[2 * a:2 * a + 2].reshape(128, 1024)), (128, 128)))[0:8]
@@ -175,6 +187,7 @@
             weights[b * 128:b * 128 + 128, a * 128:a * 128 + 128] = high
             weights[b * 128:b * 128 + 128, a * 128 + 384:a * 128 + 512] = low
             weights[b * 128:b * 128 + 128, a * 128 + 768:a * 128 + 896] = high
+    loads[2].wait()
     for b in range(8):
         lanes = slice(b * 128, min(b * 128 + 128, classes))
         block = turn(jnp.concatenate([
@@ -182,6 +195,7 @@
         ], axis=0))
         code([lambda: block[0:64]], wanted.at[2 * b])
         code([lambda: block[64:128]], wanted.at[2 * b + 1])
+    loads[3].wait()
     for q in range(16):
         inverse[q] = block_inverse[local[q // 8], (q % 8) * 8:(q % 8) * 8 + 8, :]
     own_offer.wait()
@@ -393,7 +407,9 @@
     for t in range(8):
         value = jnp.concatenate([decode(last_all.at[2 * t], 64), decode(last_all.at[2 * t + 1], 64)], axis=0)
         lanes = min(128, classes - t * 128)
-        out[:, t * 128:t * 128 + lanes] = jnp.transpose(value)[:, 0:lanes]
+        value = jnp.transpose(value)
+        out_1[:, t * 128:t * 128 + lanes] = value[0:64, 0:lanes]
+        out_2[:, t * 128:t * 128 + lanes] = value[64:128, 0:lanes]
     for copies in started:
         sent(copies)
 
@@ -410,10 +426,14 @@
     i16, bf16 = jnp.int16, jnp.bfloat16
     return pl.pallas_call(
         main_kernel,
-        out_shape=jax.ShapeDtypeStruct((128, coeffs.shape[2]), F32),
-        in_specs=[pl.BlockSpec(memory_space=pltpu.SMEM), VMEM, VMEM, VMEM, VMEM],
-        out_specs=VMEM,
+        out_shape=[jax.ShapeDtypeStruct((64, coeffs.shape[2]), F32)] * 2 + [jax.ShapeDtypeStruct((16, 128), F32)],
+        in_specs=[pl.BlockSpec(memory_space=pltpu.SMEM), ANY, ANY, ANY, ANY],
+        out_specs=[VMEM] * 3,
         scratch_shapes=[
+            pltpu.VMEM(points.shape, bf16),
+            pltpu.VMEM(targets.shape, bf16),
+            pltpu.VMEM(coeffs.shape, F32),
+            pltpu.VMEM(block_inverse.shape, F32),
             pltpu.VMEM((16, 16, 512), bf16),
             pltpu.VMEM((16, 8, 1024), F32),
             pltpu.VMEM((16, 16, 512), bf16),
@@ -451,23 +471,17 @@
             pltpu.VMEM((1024, 1024), bf16),
             pltpu.VMEM((1024, 1024), bf16),
             pltpu.VMEM((128, 1024), F32),
-            DMA((160,)), DMA((160,)), DMA((4,)),
+            DMA((160,)), DMA((160,)), DMA((4,)), DMA((4,)),
         ],
         compiler_params=pltpu.CompilerParams(collective_id=collective_id, has_side_effects=True, vmem_limit_bytes=56 * 2**20),
     )(order, points, targets, coeffs, block_inverse)
 
 
 def on_device(points, targets, coeffs, block_inverse, block_order):
-    blocks_here, per_col, _ = points.shape
-    classes = targets.shape[2]
-    deltas = main(block_order, points, targets, coeffs, block_inverse, 0)
-    deltas = deltas.reshape(2, per_col, classes)
-
-    block = lax.axis_index("row") * blocks_here + lax.broadcasted_iota(jnp.int32, (blocks_here, 1, 1), 0)
-    current = coeffs
-    for step in range(2):
-        current = jnp.where(block == block_order[step], current + deltas[step][None], current)
-    return current
+    blocks_here = points.shape[0]
+    change_1, change_2, hit = main(block_order, points, targets, coeffs, block_inverse, 0)
+    hit = hit.reshape(2, 8, 128)[:, :blocks_here, 0:1, None] > 0
+    return jnp.where(hit[0], coeffs + change_1[None], jnp.where(hit[1], coeffs + change_2[None], coeffs))
 
 
 def solution(mesh):

time: 123 us -> 119 us (0.967)
  Pallas kernels: 117 us -> 115 us
  local copies, waits for them, and re-layouts: 2.39 us -> 0.8 us
    slice x2 -> x0, local copies, waits for them, and re-layouts: 2.38 us -> none  [the longest x1 1.31 us: on_device(): block_order[step]]
    pallas_call x1, Pallas kernels: 117 us -> 115 us  [main(): pl.pallas_call(main_kernel, out_shape=[jax.ShapeDtypeStruct((64, coeffs.s...]
    eq x1 -> x0, other arithmetic: 1.26 us -> none  [on_device(): block == block_order[step]]
where the time goes in v5:
time: 119 us
  Pallas kernels  115 us (97%)
  other arithmetic  2.64 us (2%)
    pallas_call x1, Pallas kernels, main(): pl.pallas_call(main_kernel, out_shape=[jax.ShapeDtypeStruct((64, coeffs.s...  115 us
    select_n x1, other arithmetic, on_device(): jnp.where(hit[0], coeffs + change_1[None], jnp.where(hit[1], coeffs + cha...  2.63 us

profile of v5, /device:TPU:1, one launch (start us, length us, event | category | flops | bytes accessed | tf_op | source)
XLA Modules:
  0.0 118.9 jit_solution(13829692674354738332)
XLA Ops:
  0.0 0.0 copy-start
  0.0 115.5 %shard_map.55 = (f32[64,1000]{1,0:T(8,128)}, f32[64,1000]{1,0:T(8,128)}, f32[16,128]{1,0:T(8,128)}) custom-call(s32[96]{0:T(128)} %order.1, bf16[6,64,1024]{2,1,0:T(8,128)(2,1)} %points_in.1, bf16[6,64,1000]{2,1,0:T(8,128)(2,1)} %targets_in.1, f32[6,64,1000]{2,1,0:T(8,128)} %coeffs_in.1, f32[6,64,1024]{2,1,0:T(8,128)} %block_inverse_in.1), custom_call_target="tpu_custom_call" | custom-call | tf_op jit(solution)/shard_map/pallas_call | solution.py:427
  115.5 0.8 copy.7
  116.3 0.0 copy-done
  116.3 2.6 %fusion = f32[6,64,1000]{2,1,0:T(8,128)} fusion(f32[6,64,1000]{2,1,0:T(8,128)S(1)} %copy-done, f32[64,1000]{1,0:T(8,128)} %get-tuple-element.10, f32[64,1000]{1,0:T(8,128)} %get-tuple-element.9, pred[6]{0:T(512)(128)(4,1)S(1)} %get-tuple-element.12, pred[6]{0:T(512)(128)(4,1)S(1)} %get-tuple-element.11), kind=kLoop, calls=%fused_computation.1 | loop fusion | flops 1536000 | bytes 3584012 | tf_op jit(solution)/shard_map/jit(_where)/select_n | solution.py:484
  (2 shorter events, 0.0 us)
Async XLA Ops:
  0.0 116.3 %copy-start = (f32[6,64,1000]{2,1,0:T(8,128)S(1)}, f32[6,64,1000]{2,1,0:T(8,128)}, u32[]{:S(2)}) copy-start(f32[6,64,1000]{2,1,0:T(8,128)} %coeffs_in.1) | copy-start | bytes 4608004

commit v6 on v5

--- a/solution.py
+++ b/solution.py
@@ -58,7 +58,9 @@
 
 def send_all(group, source, target, send_sem, recv_sem):
     copies = []
-    for step in range(1, group.size):
+    turn_of = min(group.size, 8)
+    far_first = sorted(range(1, group.size), key=lambda step: -min(step % turn_of, turn_of - step % turn_of))
+    for step in far_first:
         to = group.after(step)
         out = pltpu.make_async_remote_copy(
             src_ref=source(to), dst_ref=target(group.me, step), send_sem=send_sem(step), recv_sem=recv_sem(step),
@@ -302,17 +304,25 @@
                 code([summed(quarter, t, gy.after(step)) for t in range(2)], y_out.at[step - 1, low])
                 y_copy(step, low).start()
 
-    for quarter in range(4):
+    def cross_quarter(quarter):
         result = products(1 - core, quarter)
         for i in range(8):
             apart[i] = result[:, i * 128:i * 128 + 128]
         code([lambda i=i: apart[i] for i in range(8)], theirs.at[quarter])
         crossing(quarter).start()
-    for quarter in range(4):
+
+    def own_quarter(quarter):
         result = products(core, quarter)
         for i in range(8):
             mine[quarter, i // 4, i % 4] = result[:, i * 128:i * 128 + 128]
-        leave_quarter(quarter)
+
+    cross_quarter(0)
+    own_quarter(0)
+    for quarter in range(1, 4):
+        cross_quarter(quarter)
+        leave_quarter(quarter - 1)
+        own_quarter(quarter)
+    leave_quarter(3)
 
     for slot in range(3):
         x_copy(gx.after(slot + 1), slot).wait_recv()

time: 119 us -> 115 us (0.966)
  Pallas kernels: 115 us -> 112 us
    pallas_call x1, Pallas kernels: 115 us -> 112 us  [main(): pl.pallas_call(main_kernel, out_shape=[jax.ShapeDtypeStruct((64, coeffs.s...]
where the time goes in v6:
time: 115 us
  Pallas kernels  112 us (97%)
  other arithmetic  2.64 us (2%)
    pallas_call x1, Pallas kernels, main(): pl.pallas_call(main_kernel, out_shape=[jax.ShapeDtypeStruct((64, coeffs.s...  112 us
    select_n x1, other arithmetic, on_device(): jnp.where(hit[0], coeffs + change_1[None], jnp.where(hit[1], coeffs + cha...  2.63 us

profile of v6, /device:TPU:1, one launch (start us, length us, event | category | flops | bytes accessed | tf_op | source)
XLA Modules:
  0.0 115.2 jit_solution(7130310225315797657)
XLA Ops:
  0.0 0.0 copy-start
  0.0 111.7 %shard_map.55 = (f32[64,1000]{1,0:T(8,128)}, f32[64,1000]{1,0:T(8,128)}, f32[16,128]{1,0:T(8,128)}) custom-call(s32[96]{0:T(128)} %order.1, bf16[6,64,1024]{2,1,0:T(8,128)(2,1)} %points_in.1, bf16[6,64,1000]{2,1,0:T(8,128)(2,1)} %targets_in.1, f32[6,64,1000]{2,1,0:T(8,128)} %coeffs_in.1, f32[6,64,1024]{2,1,0:T(8,128)} %block_inverse_in.1), custom_call_target="tpu_custom_call" | custom-call | tf_op jit(solution)/shard_map/pallas_call | solution.py:437
  111.7 0.8 copy.7
  112.5 0.0 copy-done
  112.5 2.6 %fusion = f32[6,64,1000]{2,1,0:T(8,128)} fusion(f32[6,64,1000]{2,1,0:T(8,128)S(1)} %copy-done, f32[64,1000]{1,0:T(8,128)} %get-tuple-element.10, f32[64,1000]{1,0:T(8,128)} %get-tuple-element.9, pred[6]{0:T(512)(128)(4,1)S(1)} %get-tuple-element.12, pred[6]{0:T(512)(128)(4,1)S(1)} %get-tuple-element.11), kind=kLoop, calls=%fused_computation.1 | loop fusion | flops 1536000 | bytes 3584012 | tf_op jit(solution)/shard_map/jit(_where)/select_n | solution.py:494
  (2 shorter events, 0.0 us)
Async XLA Ops:
  0.0 112.5 %copy-start = (f32[6,64,1000]{2,1,0:T(8,128)S(1)}, f32[6,64,1000]{2,1,0:T(8,128)}, u32[]{:S(2)}) copy-start(f32[6,64,1000]{2,1,0:T(8,128)} %coeffs_in.1) | copy-start | bytes 4608004

commit v7 on v6

--- a/solution.py
+++ b/solution.py
@@ -45,10 +45,15 @@
         return lax.rem(self.me + self.size - step, self.size)
 
 
+def far_first(size):
+    turn_of = min(size, 8)
+    return sorted(range(1, size), key=lambda step: -min(step % turn_of, turn_of - step % turn_of))
+
+
 def signal_all(groups):
     barrier = pltpu.get_barrier_semaphore()
     for group in groups:
-        for step in range(1, group.size):
+        for step in far_first(group.size):
             pl.semaphore_signal(barrier, inc=1, device_id=group.at(group.after(step)), device_id_type=MESH)
 
 
@@ -58,9 +63,7 @@
 
 def send_all(group, source, target, send_sem, recv_sem):
     copies = []
-    turn_of = min(group.size, 8)
-    far_first = sorted(range(1, group.size), key=lambda step: -min(step % turn_of, turn_of - step % turn_of))
-    for step in far_first:
+    for step in far_first(group.size):
         to = group.after(step)
         out = pltpu.make_async_remote_copy(
             src_ref=source(to), dst_ref=target(group.me, step), send_sem=send_sem(step), recv_sem=recv_sem(step),
@@ -300,7 +303,7 @@
                     code([summed(quarter, high, t) for t in range(4)], x_out.at[slot])
                     x_copy(to, slot).start()
         else:
-            for step in range(1, 4):
+            for step in (2, 1, 3):
                 code([summed(quarter, t, gy.after(step)) for t in range(2)], y_out.at[step - 1, low])
                 y_copy(step, low).start()
 

time: 115 us -> 115 us (level)
  no operation moved by 1% of the time
where the time goes in v7:
time: 115 us
  Pallas kernels  112 us (97%)
  other arithmetic  2.64 us (2%)
    pallas_call x1, Pallas kernels, main(): pl.pallas_call(main_kernel, out_shape=[jax.ShapeDtypeStruct((64, coeffs.s...  112 us
    select_n x1, other arithmetic, on_device(): jnp.where(hit[0], coeffs + change_1[None], jnp.where(hit[1], coeffs + cha...  2.63 us

profile of v7, /device:TPU:1, one launch (start us, length us, event | category | flops | bytes accessed | tf_op | source)
XLA Modules:
  0.0 115.2 jit_solution(1078042722239990312)
XLA Ops:
  0.0 0.0 copy-start
  0.0 111.8 %shard_map.55 = (f32[64,1000]{1,0:T(8,128)}, f32[64,1000]{1,0:T(8,128)}, f32[16,128]{1,0:T(8,128)}) custom-call(s32[96]{0:T(128)} %order.1, bf16[6,64,1024]{2,1,0:T(8,128)(2,1)} %points_in.1, bf16[6,64,1000]{2,1,0:T(8,128)(2,1)} %targets_in.1, f32[6,64,1000]{2,1,0:T(8,128)} %coeffs_in.1, f32[6,64,1024]{2,1,0:T(8,128)} %block_inverse_in.1), custom_call_target="tpu_custom_call" | custom-call | tf_op jit(solution)/shard_map/pallas_call | solution.py:440
  111.8 0.8 copy.7
  112.6 0.0 copy-done
  112.6 2.6 %fusion = f32[6,64,1000]{2,1,0:T(8,128)} fusion(f32[6,64,1000]{2,1,0:T(8,128)S(1)} %copy-done, f32[64,1000]{1,0:T(8,128)} %get-tuple-element.10, f32[64,1000]{1,0:T(8,128)} %get-tuple-element.9, pred[6]{0:T(512)(128)(4,1)S(1)} %get-tuple-element.12, pred[6]{0:T(512)(128)(4,1)S(1)} %get-tuple-element.11), kind=kLoop, calls=%fused_computation.1 | loop fusion | flops 1536000 | bytes 3584012 | tf_op jit(solution)/shard_map/jit(_where)/select_n | solution.py:497
  (2 shorter events, 0.0 us)
Async XLA Ops:
  0.0 112.6 %copy-start = (f32[6,64,1000]{2,1,0:T(8,128)S(1)}, f32[6,64,1000]{2,1,0:T(8,128)}, u32[]{:S(2)}) copy-start(f32[6,64,1000]{2,1,0:T(8,128)} %coeffs_in.1) | copy-start | bytes 4608004
